TPU v7x, 256 devices: a whole 4x4x8 slice. The times are simulated.
256 devices in a mesh: tile: 64 (over z, x, core), occ: 4 (over y).
Axes of the slice: x: 4, y: 4, z: 8, core: 2. Of those that a mesh axis runs over, the one named last changes fastest.
Arguments:
- amplitudes: bfloat16 [8, 512, 128, 128], P('occ', 'tile'), may hold values from -6 to 6
- exchange_ints: bfloat16 [8, 512, 128, 128], P('occ', 'tile'), may hold values from -6 to 6
- left_factors: bfloat16 [1024, 128, 128], P('tile'), may hold values from -0.5 to 0.5
- right_factors: bfloat16 [1024, 128, 128], P('tile'), may hold values from -0.1875 to 0.1875
- ladder_sources: int32 [2048, 8], P('tile'), may hold values from 0 to 7
- ladder_factors: int32 [2048, 8], P('tile'), may hold values from 0 to 15
- dest_owners: int32 [2048, 1], P('tile'), may hold values from 0 to 63; in each aligned block of 32 rows (0 to 31, 32 to 63, ...) at most 2 rows name the same one
- dest_slots: int32 [2048], P('tile'), may hold values from 0 to 7
- cycle_blocks: int32 [512], P('tile'), may hold values from 0 to 1
- cycle_ints: bfloat16 [128, 1024, 1024], P('tile', 'occ'), may hold values from -0.1875 to 0.1875
Outputs:
- residual: bfloat16 [8, 512, 128, 128], P('occ', 'tile')
Inputs may be any that keep to these rules, and one draw needn't show every extreme that they name: `dest_owners`: among the rows of one tile index, at most 2 name the same owner, a bound that some block reaches.
All inputs are finite; a program needn't handle non-finite values.
Results may differ from a plain program's by a relative error of at most 0.0053.
Values may be sent and summed in bfloat16 or wider, within the bound.
A program may use at most 128 MiB of HBM per device.

v0:
```python
import jax
import jax.numpy as jnp
from jax import lax
from jax.sharding import PartitionSpec as P


def pack_tiles(sending, dest_slots, owners, ranking, first_rank, width, n_tile):
    occ_here = sending.shape[1]
    tile_width = sending.shape[2]
    inside = (ranking >= first_rank) & (ranking < first_rank + width)
    limit = n_tile * width
    places = jnp.where(inside, owners * width + ranking - first_rank, limit)
    buffer = (
        jnp.zeros((limit, occ_here, tile_width, tile_width), jnp.bfloat16)
        .at[places]
        .set(sending, mode="drop")
    )
    labels = jnp.full((limit,), -1, jnp.int32).at[places].set(dest_slots, mode="drop")
    return (
        buffer.reshape(n_tile, width, occ_here, tile_width, tile_width),
        labels.reshape(n_tile, width),
    )


def sum_by_label(received, got_labels, slots_here):
    occ_here = received.shape[2]
    tile_width = received.shape[3]
    selector = (
        got_labels.reshape(-1)[:, None] == jnp.arange(slots_here, dtype=jnp.int32)[None, :]
    ).astype(jnp.bfloat16)
    return jnp.einsum(
        "ms,mjab->jsab",
        selector,
        received.reshape(-1, occ_here, tile_width, tile_width),
        preferred_element_type=jnp.float32,
    )


def local(
    amplitudes,
    exchange_ints,
    left_factors,
    right_factors,
    ladder_sources,
    ladder_factors,
    dest_owners,
    dest_slots,
    cycle_blocks,
    cycle_ints,
):
    occ_here = amplitudes.shape[0]
    slots_here = amplitudes.shape[1]
    tile_width = amplitudes.shape[2]
    terms_here = ladder_sources.shape[0]
    products = ladder_sources.shape[1]
    n_tile = lax.axis_size("tile")
    capacity = max(2, 2 * terms_here // n_tile)
    partial_value = jnp.zeros((terms_here, occ_here, tile_width, tile_width), jnp.float32)
    group_width = 4
    for group_start in range(0, products, group_width):
        group_stop = min(products, group_start + group_width)
        factor_ids = ladder_factors[:, group_start:group_stop]
        left_tiles = jnp.take(left_factors, factor_ids, axis=0)
        amp_tiles = jnp.take(amplitudes, ladder_sources[:, group_start:group_stop], axis=1)
        half_prod = jnp.einsum(
            "gqac,jgqcd->gqjad", left_tiles, amp_tiles, preferred_element_type=jnp.float32
        ).astype(jnp.bfloat16)
        right_tiles = jnp.take(right_factors, factor_ids, axis=0)
        partial_value = partial_value + jnp.einsum(
            "gqjad,gqbd->gjab", half_prod, right_tiles, preferred_element_type=jnp.float32
        )
    sending = partial_value.astype(jnp.bfloat16)
    owners = dest_owners[:, 0]
    term_order = jnp.arange(terms_here, dtype=jnp.int32)
    same_owner = owners[:, None] == owners[None, :]
    earlier = term_order[:, None] > term_order[None, :]
    ranking = jnp.sum((same_owner & earlier).astype(jnp.int32), axis=1)
    buffer, labels = pack_tiles(sending, dest_slots, owners, ranking, 0, capacity, n_tile)
    received, got_labels = (
        lax.all_to_all(buffer, "tile", split_axis=0, concat_axis=0, tiled=True),
        lax.all_to_all(labels, "tile", split_axis=0, concat_axis=0, tiled=True),
    )
    ladder = sum_by_label(received, got_labels, slots_here)
    amp_matrix = amplitudes.transpose(1, 2, 0, 3).reshape(
        slots_here, tile_width, occ_here * tile_width
    )
    chosen = jnp.take(cycle_ints, cycle_blocks, axis=0)
    product = jnp.einsum("sak,skn->san", amp_matrix, chosen, preferred_element_type=jnp.float32)
    cycle_part = lax.psum_scatter(
        product.reshape(
            slots_here, tile_width, occ_here * lax.axis_size("occ"), tile_width
        ).transpose(2, 0, 1, 3),
        "occ",
        scatter_dimension=0,
        tiled=True,
    )
    return (exchange_ints.astype(jnp.float32) + ladder + cycle_part).astype(jnp.bfloat16)


def solution(mesh):
    placed = (
        P("occ", "tile", None, None),
        P("occ", "tile", None, None),
        P("tile", None, None),
        P("tile", None, None),
        P("tile", None),
        P("tile", None),
        P("tile", None),
        P("tile"),
        P("tile"),
        P("tile", "occ", None),
    )
    return jax.shard_map(
        local, mesh=mesh, in_specs=placed, out_specs=P("occ", "tile", None, None), check_vma=False
    )
```

profile of v0, /device:TPU:1, one launch (start us, length us, event | category | flops | bytes accessed | tf_op | source)
XLA Modules:
  0.0 341.0 jit_solution(11197274263891753121)
XLA Ops:
  6.5 0.0 copy-start
  6.5 0.9 convert_reduce_fusion
  7.5 0.7 fusion.68
  8.1 0.8 scatter_custom_fusion.1
  9.0 0.8 all_to_all.10
  9.7 13.0 %all-to-all-start.1 = ((s32[64,1,2]{2,1,0:T(1,128)}), s32[64,1,2]{2,1,0:T(1,128)S(1)}, u32[]{:S(2)}, u32[]{:S(2)}) async-start(s32[64,1,2]{2,1,0:T(1,128)} %bitcast.27), calls=%async_computation.1 | async-start | bytes 65536 | tf_op jit(solution)/shard_map/all_to_all | solution.py:81
  22.7 0.8 compare_select_fusion.3
  23.5 0.8 compare_and_fusion.3
  24.2 0.8 compare_select_fusion.2
  25.0 0.8 compare_and_fusion.2
  25.8 0.1 copy.83
  25.9 0.1 reshape.152
  26.0 0.0 copy-start.3
  26.0 4.1 %gather_fusion.5 = bf16[128,128,128]{2,1,0:T(8,128)(2,1)} fusion(bf16[16,128,128]{2,1,0:T(8,128)(2,1)} %param.16, s32[1024]{0:T(1024)S(1)} %pad_clamp_fusion.1), kind=kCustom, calls=%fused_computation.4.clone | custom fusion | bytes 8389120 | tf_op jit(solution)/shard_map/jit(_take)/gather | solution.py:63
  30.1 0.0 copy-done.3
  30.1 0.0 copy-start.2
  30.1 3.1 gather_fusion.6
  33.3 0.1 copy.75
  33.4 0.1 reshape.140
  33.5 0.0 copy-done.2
  33.5 3.0 gather_fusion.2
  36.5 0.0 copy-start.1
  36.5 3.0 gather_fusion.3
  39.6 0.1 copy.80
  39.6 0.1 reshape.148
  39.8 0.0 copy-done.1
  39.8 6.5 %gather_fusion.4 = bf16[128,2,128,128]{3,2,1,0:T(8,128)(2,1)} fusion(bf16[2,8,128,128]{3,2,1,0:T(8,128)(2,1)S(1)} %copy-done.1, s32[1024]{0:T(1024)S(1)} %pad_clamp_fusion.2), kind=kCustom, calls=%fused_computation.2.clone | custom fusion | bytes 16777728 | tf_op jit(solution)/shard_map/jit(_take)/gather | solution.py:64
  46.3 11.9 %copy.81 = bf16[32,4,2,128,128]{3,4,1,2,0:T(8,128)(2,1)} copy(bf16[32,4,2,128,128]{4,3,2,1,0:T(8,128)(2,1)} %bitcast.100) | data formatting | bytes 16777216 | tf_op jit(solution)/shard_map/jit(_take)/gather | solution.py:64
  58.2 0.1 copy.79
  58.3 0.1 copy.82
  58.5 0.1 copy.72
  58.5 0.1 reshape.136
  58.7 6.5 %gather_fusion.1 = bf16[128,2,128,128]{3,2,1,0:T(8,128)(2,1)} fusion(bf16[2,8,128,128]{3,2,1,0:T(8,128)(2,1)S(1)} %copy-done.1, s32[1024]{0:T(1024)S(1)} %pad_clamp_fusion.4), kind=kCustom, calls=%fused_computation.clone | custom fusion | bytes 16777728 | tf_op jit(solution)/shard_map/jit(_take)/gather | solution.py:64
  65.2 12.0 %copy.73 = bf16[32,4,2,128,128]{3,4,1,2,0:T(8,128)(2,1)} copy(bf16[32,4,2,128,128]{4,3,2,1,0:T(8,128)(2,1)} %bitcast.101) | data formatting | bytes 16777216 | tf_op jit(solution)/shard_map/jit(_take)/gather | solution.py:64
  77.1 0.1 copy.71
  77.2 0.1 copy.74
  77.4 9.7 %fusion = f32[32,2,128,128,1]{3,2,4,1,0:T(8,128)} fusion(bf16[32,4,2,128,128]{3,4,1,2,0:T(8,128)(2,1)} %copy.81, pred[32,4]{1,0:T(8,128)(4,1)S(1)} %copy.79, bf16[32,4,128,128]{3,2,1,0:T(8,128)(2,1)} %bitcast.105, bf16[32,4,128,128]{3,2,1,0:T(8,128)(2,1)} %bitcast.104, pred[32,4]{1,0:T(8,128)(4,1)S(1)} %copy.82), kind=kOutput, calls=%fused_computation.9 | convolution fusion | flops 2160066560 | bytes 20971776 | tf_op jit(solution)/shard_map/gqjad,gqbd->gjab/dot_general | solution.py:69
  87.1 10.5 %fusion.30 = bf16[32,2,128,128]{3,2,1,0:T(8,128)(2,1)} fusion(f32[32,2,128,128,1]{3,2,4,1,0:T(8,128)} %fusion, bf16[32,4,128,128]{3,2,1,0:T(8,128)(2,1)} %bitcast.107, pred[32,4]{1,0:T(8,128)(4,1)S(1)} %copy.74, bf16[32,4,2,128,128]{3,4,1,2,0:T(8,128)(2,1)} %copy.73, pred[32,4]{1,0:T(8,128)(4,1)S(1)} %copy.71, bf16[32,4,128,128]{3,2,1,0:T(8,128)(2,1)} %bitcast.106), kind=kOutput, calls=%fused_computation.28 | convolution fusion | flops 2162163712 | bytes 23068928 | tf_op jit(solution)/shard_map/gqjad,gqbd->gjab/dot_general | solution.py:69
  97.6 5.3 %broadcast_in_dim.45 = bf16[128,2,128,128]{3,2,1,0:T(8,128)(2,1)} broadcast(bf16[]{:T(256)} %constant.23.clone.1), dimensions={} | broadcast | bytes 8388610 | tf_op jit(solution)/shard_map/broadcast_in_dim | solution.py:14
  102.9 6.3 %scatter_fusion = bf16[128,2,128,128]{3,2,1,0:T(8,128)(2,1)} fusion(bf16[128,2,128,128]{3,2,1,0:T(8,128)(2,1)} %broadcast_in_dim.45, s32[32]{0:T(128)S(1)} %fusion.68, bf16[32,2,128,128]{3,2,1,0:T(8,128)(2,1)} %fusion.30), kind=kCustom, calls=%fused_computation.7 | custom fusion | bytes 6291584 | tf_op jit(solution)/shard_map/scatter | solution.py:16
  109.2 16.3 %copy.87 = bf16[64,2,2,128,128]{4,1,3,2,0:T(2,128)(2,1)} copy(bf16[64,2,2,128,128]{4,3,2,1,0:T(8,128)(2,1)} %bitcast.99) | data formatting | bytes 16777216 | tf_op jit(solution)/shard_map/reshape | solution.py:20
  125.5 0.0 copy-start.5
  125.5 0.0 all-to-all-done.1
  125.5 10.5 %all-to-all-start = ((bf16[64,2,2,128,128]{4,1,3,2,0:T(2,128)(2,1)}), bf16[64,2,2,128,128]{4,1,3,2,0:T(2,128)(2,1)}, u32[]{:S(2)}, u32[]{:S(2)}) async-start(bf16[64,2,2,128,128]{4,1,3,2,0:T(2,128)(2,1)} %copy.87), calls=%async_computation | async-start | bytes 16777216 | tf_op jit(solution)/shard_map/all_to_all | solution.py:80
  136.0 0.0 reduce-scatter.2.cloned.1.call-start
  136.0 0.3 copy.90
  136.3 0.0 copy-done.5
  136.4 0.0 copy-done
  136.4 2.8 gather_fusion
  139.1 5.7 %fusion.41 = f32[8,1024,128]{2,1,0:T(8,128)} fusion(bf16[8,128,256]{1,2,0:T(8,128)(2,1)S(1)} %bitcast.109, bf16[8,256,1024]{2,1,0:T(8,128)(2,1)} %gather_fusion, pred[8]{0:T(512)(128)(4,1)S(1)} %compare_and_fusion.4), kind=kOutput, calls=%fused_computation.35 | convolution fusion | flops 538968064 | bytes 8912904 | tf_op jit(solution)/shard_map/sak,skn->san/dot_general | solution.py:88
  144.8 5.4 %copy.93 = f32[8,128,8,128]{3,0,1,2:T(8,128)} copy(f32[8,128,8,128]{1,3,2,0:T(8,128)} %bitcast.108) | data formatting | bytes 8388608 | tf_op jit(solution)/shard_map/reshape | solution.py:90
  150.2 0.0 reduce-scatter.2.cloned.1.call-update
  150.2 0.5 broadcast.107
  150.7 0.7 reduce.3
  151.5 0.1 eq.34
  151.6 0.0 copy-start.4
  151.6 166.8 %all-to-all-done = bf16[64,2,2,128,128]{4,1,3,2,0:T(2,128)(2,1)} async-done(((bf16[64,2,2,128,128]{4,1,3,2,0:T(2,128)(2,1)}), bf16[64,2,2,128,128]{4,1,3,2,0:T(2,128)(2,1)}, u32[]{:S(2)}, u32[]{:S(2)}) %all-to-all-start) | async-done | bytes 8388640 | tf_op jit(solution)/shard_map/all_to_all | solution.py:80
  318.4 10.0 %copy.88 = bf16[64,2,2,128,128]{4,1,0,3,2:T(2,128)(2,1)} copy(bf16[64,2,2,128,128]{4,1,3,2,0:T(2,128)(2,1)} %all-to-all-done) | data formatting | bytes 16777216 | tf_op jit(solution)/shard_map/all_to_all | solution.py:80
  328.4 0.0 reduce-scatter.2.cloned.1.call-done
  328.4 0.0 copy-done.4
  328.4 4.8 %fusion.63 = bf16[2,8,128,128]{3,1,2,0:T(8,128)(2,1)S(1)} fusion(f32[2,8,128,128]{3,1,2,0:T(8,128)} %reduce-scatter.2.cloned.1.call-done, bf16[128,2,128,128]{3,0,2,1:T(8,128)(2,1)} %bitcast.102, bf16[2,8,128,128]{3,2,1,0:T(8,128)(2,1)S(1)} %copy-done.4, s32[128]{0:T(128)S(1)} %eq.34), kind=kOutput, calls=%fused_computation.46 | convolution fusion | flops 68158464 | bytes 10486272 | tf_op jit(solution)/shard_map/ms,mjab->jsab/dot_general | solution.py:31
  333.2 0.9 copy.94
  (7 shorter events, 0.0 us)
Async XLA Ops:
  6.5 129.8 %copy-start = (bf16[2,256,1024]{2,1,0:T(8,128)(2,1)S(1)}, bf16[2,256,1024]{2,1,0:T(8,128)(2,1)}, u32[]{:S(2)}) copy-start(bf16[2,256,1024]{2,1,0:T(8,128)(2,1)} %param.23) | copy-start | bytes 3145732
  9.7 115.8 %all-to-all-start.1 = ((s32[64,1,2]{2,1,0:T(1,128)}), s32[64,1,2]{2,1,0:T(1,128)S(1)}, u32[]{:S(2)}, u32[]{:S(2)}) async-start(s32[64,1,2]{2,1,0:T(1,128)} %bitcast.27), calls=%async_computation.1 | async-start | bytes 65536 | tf_op jit(solution)/shard_map/all_to_all | solution.py:81
  26.0 4.2 %copy-start.3 = (bf16[16,128,128]{2,1,0:T(8,128)(2,1)S(1)}, bf16[16,128,128]{2,1,0:T(8,128)(2,1)}, u32[]{:S(2)}) copy-start(bf16[16,128,128]{2,1,0:T(8,128)(2,1)} %param.17) | copy-start | bytes 1572868
  30.1 3.4 copy-start.2
  36.5 3.2 copy-start.1
  125.5 10.8 %copy-start.5 = (s32[8]{0:T(128)S(1)}, s32[8]{0:T(128)}, u32[]{:S(2)}) copy-start(s32[8]{0:T(128)} %param.22) | copy-start | bytes 100
  125.5 192.9 %all-to-all-start = ((bf16[64,2,2,128,128]{4,1,3,2,0:T(2,128)(2,1)}), bf16[64,2,2,128,128]{4,1,3,2,0:T(2,128)(2,1)}, u32[]{:S(2)}, u32[]{:S(2)}) async-start(bf16[64,2,2,128,128]{4,1,3,2,0:T(2,128)(2,1)} %copy.87), calls=%async_computation | async-start | bytes 16777216 | tf_op jit(solution)/shard_map/all_to_all | solution.py:80
  136.0 192.4 %reduce-scatter.2.cloned.1.call-start = ((), (), s32[]{:S(2)}) async-start(), calls=%async_computation.3 | async-start | bytes 5242880 | tf_op jit(solution)/shard_map/reduce_scatter | solution.py:89
  151.6 176.8 %copy-start.4 = (bf16[2,8,128,128]{3,2,1,0:T(8,128)(2,1)S(1)}, bf16[2,8,128,128]{3,2,1,0:T(8,128)(2,1)}, u32[]{:S(2)}) copy-start(bf16[2,8,128,128]{3,2,1,0:T(8,128)(2,1)} %param.15) | copy-start | bytes 1572868
Sparse Core Ops, SparseCore 0:
  150.3 50.5 reduce-scatter.1
where the time goes:
time: 345 us; the launch traced here: 341 us
  waiting for transfers between devices  167 us (48%)
  local copies, waits for them, and re-layouts  101 us (29%)
  matrix products  30.8 us (9%)
  starting transfers between devices  23.5 us (7%)
  between operations  13.6 us (4%)
  other arithmetic  5.45 us (2%)
    all_to_all x1, waiting for transfers between devices, local(): lax.all_to_all(buffer, 'tile', split_axis=0, concat_axis=0, tiled=True)  167 us
    gather x4, local copies, waits for them, and re-layouts, local(): jnp.take(amplitudes, ladder_sources[:, group_start:group_stop], axis=1)  37 us
    dot_general x2, matrix products, local(): jnp.einsum('gqjad,gqbd->gjab', half_prod, right_tiles, preferred_element_...  20.2 us
    reshape x1, local copies, waits for them, and re-layouts, pack_tiles(): buffer.reshape(n_tile, width, occ_here, tile_width, tile_width)  16.3 us
    all_to_all x1, starting transfers between devices, local(): lax.all_to_all(labels, 'tile', split_axis=0, concat_axis=0, tiled=True)  13 us
    all_to_all x1, starting transfers between devices, local(): lax.all_to_all(buffer, 'tile', split_axis=0, concat_axis=0, tiled=True)  10.5 us
    all_to_all x1, local copies, waits for them, and re-layouts, local(): lax.all_to_all(buffer, 'tile', split_axis=0, concat_axis=0, tiled=True)  10 us
    gather x2, local copies, waits for them, and re-layouts, local(): left_tiles = jnp.take(left_factors, factor_ids, axis=0)  7.16 us
  transfers between devices with their start and end apart: 3, of which 1 were waited for; matrix products, arithmetic and copies ran while one was open for 38% of the time, Pallas kernels for 0%

commit v1 on v0

v1 whole, which is shorter than its diff:
```python
import functools

import jax
import jax.numpy as jnp
from jax import lax
from jax.experimental import pallas as pl
from jax.experimental.pallas import tpu as pltpu
from jax.sharding import PartitionSpec as P

MESH = pl.DeviceIdType.MESH
NZ, NX, NC = 8, 4, 2
TERMS = 32
SLOTS = 8
TW = 128
J = 2
ROWS = 32
PARTS = TW // ROWS
CHUNKS = J * PARTS
RING = 5
SMALL_CAP, SMALL_ENTRIES = 14, 80


def cycle_kernel(blocks_ref, amp_ref, ints_ref, out_ref):
    def one(s, _):
        ints = ints_ref.at[blocks_ref[s]]
        rows = jnp.concatenate([amp_ref[0, s], amp_ref[1, s]], axis=1)
        prod = jnp.dot(rows, ints[...], preferred_element_type=jnp.float32)
        for j in range(8):
            out_ref[j, s] = prod[:, j * TW : (j + 1) * TW].astype(jnp.bfloat16)
        return 0

    lax.fori_loop(0, SLOTS, one, 0)


def cycle_products(cycle_blocks, amplitudes, cycle_ints):
    vmem = pl.BlockSpec(memory_space=pltpu.VMEM)
    return pl.pallas_call(
        cycle_kernel,
        out_shape=jax.ShapeDtypeStruct((8, SLOTS, TW, TW), jnp.bfloat16),
        in_specs=[pl.BlockSpec(memory_space=pltpu.SMEM), vmem, vmem],
        out_specs=vmem,
        compiler_params=pltpu.CompilerParams(vmem_limit_bytes=32 * 2**20),
        cost_estimate=pl.CostEstimate(
            flops=2 * SLOTS * TW * 256 * 1024, bytes_accessed=4 * 2**20, transcendentals=0
        ),
    )(cycle_blocks, amplitudes, cycle_ints)


def ladder_kernel(src_ref, fac_ref, pos_ref, amp_ref, left_ref, right_ref, out_ref, rt, stage, sem):
    for f in range(16):
        rt[f] = right_ref[f].T

    def put(g):
        return pltpu.make_async_copy(stage.at[g], out_ref.at[:, pos_ref[g]], sem.at[g])

    def one(g, _):
        acc = jnp.zeros((2 * TW, TW), jnp.float32)
        for q in range(8):
            s = src_ref[g, q]
            f = fac_ref[g, q]
            amps = jnp.concatenate([amp_ref[0, s], amp_ref[1, s]], axis=1)
            half = jnp.dot(left_ref[f], amps, preferred_element_type=jnp.float32).astype(
                jnp.bfloat16
            )
            both = jnp.concatenate([half[:, :TW], half[:, TW:]], axis=0)
            acc = acc + jnp.dot(both, rt[f], preferred_element_type=jnp.float32)
        stage[g] = acc.astype(jnp.bfloat16).reshape(J, TW, TW)
        put(g).start()
        return 0

    lax.fori_loop(0, TERMS, one, 0)

    def finish(g, _):
        put(g).wait()
        return 0

    lax.fori_loop(0, TERMS, finish, 0)


def ladder_terms(sources, factors, places, amplitudes, left, right):
    smem = pl.BlockSpec(memory_space=pltpu.SMEM)
    vmem = pl.BlockSpec(memory_space=pltpu.VMEM)
    return pl.pallas_call(
        ladder_kernel,
        out_shape=jax.ShapeDtypeStruct((J, NX * TERMS, TW, TW), jnp.bfloat16),
        in_specs=[smem, smem, smem, vmem, vmem, vmem],
        out_specs=pl.BlockSpec(memory_space=pl.ANY),
        scratch_shapes=[
            pltpu.VMEM((16, TW, TW), jnp.bfloat16),
            pltpu.VMEM((TERMS, J, TW, TW), jnp.bfloat16),
            pltpu.SemaphoreType.DMA((TERMS,)),
        ],
        compiler_params=pltpu.CompilerParams(vmem_limit_bytes=32 * 2**20),
        cost_estimate=pl.CostEstimate(
            flops=2 * 1024 * TW**3, bytes_accessed=4 * 2**20, transcendentals=0
        ),
    )(sources, factors, places, amplitudes, left, right)


def route_kernel(
    cap, entries, perm_ref, same_ref, end_ref, some_ref, p_ref, out_ref,
    recv, stage, sums, zs, zr, xs_sem, fs_sem, lx_sem, rx_sem, zs_sem, zr_sem,
):
    t = lax.axis_index("tile")
    y = lax.axis_index("occ")
    core = t % NC
    x = (t // NC) % NX
    z = t // (NC * NX)
    m = t % (NC * NX)

    def at(zz, xx, cc):
        return {"tile": (zz * NX + xx) * NC + cc, "occ": y}

    sibling = at(z, x, 1 - core)
    ups = at((z + 1) % NZ, x, core)
    downs = at((z + NZ - 1) % NZ, x, core)
    barrier = pltpu.get_barrier_semaphore()
    partners = [at(z, (x + d) % NX, core) for d in range(1, NX)] + [sibling, ups, downs]
    for partner in partners:
        pl.semaphore_signal(barrier, inc=1, device_id=partner, device_id_type=MESH)
    pl.semaphore_wait(barrier, len(partners))

    def mine(h, xx):
        return p_ref.at[h // PARTS, xx, pl.ds(0, cap), pl.ds((h % PARTS) * ROWS, ROWS)]

    def send_x(h, d):
        xx = (x + d) % NX
        return pltpu.make_async_remote_copy(
            src_ref=mine(h, xx), dst_ref=recv.at[h, m],
            send_sem=xs_sem.at[h, d], recv_sem=rx_sem.at[h, m],
            device_id=at(z, xx, core), device_id_type=MESH,
        )

    def send_own(h):
        return pltpu.make_async_remote_copy(
            src_ref=mine(h, x), dst_ref=recv.at[h, m],
            send_sem=xs_sem.at[h, 0], recv_sem=rx_sem.at[h, m],
            device_id=sibling, device_id_type=MESH,
        )

    def copy_own(h):
        return pltpu.make_async_copy(mine(h, x), recv.at[h, m], lx_sem.at[h])

    def forward(h, d):
        source = ((x + d) % NX) * NC + core
        return pltpu.make_async_remote_copy(
            src_ref=recv.at[h, source], dst_ref=recv.at[h, source],
            send_sem=fs_sem.at[h, d], recv_sem=rx_sem.at[h, source],
            device_id=sibling, device_id_type=MESH,
        )

    def arrived(h, source):
        return pltpu.make_async_copy(recv.at[h, source], recv.at[h, source], rx_sem.at[h, source])

    def start_x(h):
        for d in range(1, NX):
            send_x(h, d).start()
        send_own(h).start()
        copy_own(h).start()

    def send_z(h, way, step):
        if step == 0:
            part = pl.ds(4 * way, 4)
        else:
            part = pl.ds(0, SLOTS)
        return pltpu.make_async_remote_copy(
            src_ref=zs.at[h, way, step, part], dst_ref=zr.at[h, way, step, part],
            send_sem=zs_sem.at[h, way, step], recv_sem=zr_sem.at[h, way, step],
            device_id=ups if way == 0 else downs, device_id_type=MESH,
        )

    def own(h, zz, s):
        place = zz * SLOTS + s
        value = sums[h % RING, end_ref[place]]
        return jnp.where(some_ref[place] != 0, value, 0.0)

    def z_step(h, step):
        for way in range(2):
            if step > 0:
                send_z(h, way, step - 1).wait_recv()
            zz = (z + 4 - step) % NZ if way == 0 else (z + 4 + step) % NZ
            for s in range(4 * way, 4 * way + 4) if step == 0 else range(SLOTS):
                value = own(h, zz, s)
                if step > 1 or (step == 1 and s // 4 == way):
                    value = value + zr[h, way, step - 1, s].astype(jnp.float32)
                zs[h, way, step, s] = value.astype(jnp.bfloat16)
            send_z(h, way, step).start()

    def finish(h):
        for way in range(2):
            send_z(h, way, 3).wait_recv()
        for s in range(SLOTS):
            total = own(h, z, s) + zr[h, 0, 3, s].astype(jnp.float32)
            total = total + zr[h, 1, 3, s].astype(jnp.float32)
            out_ref[h // PARTS, s, pl.ds((h % PARTS) * ROWS, ROWS)] = total

    def collect(h):
        for d in range(1, NX):
            arrived(h, ((x + d) % NX) * NC + core).wait()
            forward(h, d).start()
        copy_own(h).wait()
        for d in range(NX):
            arrived(h, ((x + d) % NX) * NC + 1 - core).wait()
        for source in range(NX * NC):
            stage[source * cap : (source + 1) * cap] = recv[h, source]

        def entry(e, total):
            value = stage[perm_ref[e]].astype(jnp.float32)
            total = value + jnp.where(same_ref[e] != 0, total, 0.0)
            sums[h % RING, e] = total
            return total

        lax.fori_loop(0, entries, entry, jnp.zeros((ROWS, TW), jnp.float32), unroll=4)

    start_x(0)

    def turn(i, _):
        @pl.when(i + 1 < CHUNKS)
        def _():
            start_x(i + 1)

        @pl.when(i < CHUNKS)
        def _():
            collect(i)
            z_step(i, 0)

        for step in range(1, 4):
            @pl.when((i >= step) & (i - step < CHUNKS))
            def _(step=step):
                z_step(i - step, step)

        @pl.when(i >= 4)
        def _():
            finish(i - 4)

        return 0

    lax.fori_loop(0, CHUNKS + 4, turn, 0)

    def drain(h, _):
        for d in range(1, NX):
            send_x(h, d).wait_send()
            forward(h, d).wait_send()
        send_own(h).wait_send()
        for way in range(2):
            for step in range(4):
                send_z(h, way, step).wait_send()
        return 0

    lax.fori_loop(0, CHUNKS, drain, 0)


def route(cap, entries, collective_id, perm, same, end, some, packed):
    smem = pl.BlockSpec(memory_space=pltpu.SMEM)
    dma = pltpu.SemaphoreType.DMA
    return pl.pallas_call(
        functools.partial(route_kernel, cap, entries),
        out_shape=jax.ShapeDtypeStruct((J, SLOTS, TW, TW), jnp.float32),
        in_specs=[smem, smem, smem, smem, pl.BlockSpec(memory_space=pl.ANY)],
        out_specs=pl.BlockSpec(memory_space=pltpu.VMEM),
        scratch_shapes=[
            pltpu.VMEM((CHUNKS, NX * NC, cap, ROWS, TW), jnp.bfloat16),
            pltpu.VMEM((NX * NC * cap, ROWS, TW), jnp.bfloat16),
            pltpu.VMEM((RING, entries, ROWS, TW), jnp.float32),
            pltpu.VMEM((CHUNKS, 2, 4, SLOTS, ROWS, TW), jnp.bfloat16),
            pltpu.VMEM((CHUNKS, 2, 4, SLOTS, ROWS, TW), jnp.bfloat16),
            dma((CHUNKS, NX)),
            dma((CHUNKS, NX)),
            dma((CHUNKS,)),
            dma((CHUNKS, NX * NC)),
            dma((CHUNKS, 2, 4)),
            dma((CHUNKS, 2, 4)),
        ],
        compiler_params=pltpu.CompilerParams(
            collective_id=collective_id, has_side_effects=True, vmem_limit_bytes=56 * 2**20
        ),
        cost_estimate=pl.CostEstimate(
            flops=2**22, bytes_accessed=8 * 2**20, transcendentals=0
        ),
    )(perm, same, end, some, packed)


def ranks_in_column(keys):
    column = (keys // (SLOTS * NC)) % NX
    order = jnp.arange(TERMS, dtype=jnp.int32)
    earlier = order[:, None] > order[None, :]
    alike = column[..., :, None] == column[..., None, :]
    return column, jnp.sum((alike & earlier).astype(jnp.int32), axis=-1)


def local(
    amplitudes, exchange_ints, left_factors, right_factors, ladder_sources, ladder_factors,
    dest_owners, dest_slots, cycle_blocks, cycle_ints,
):
    tile = lax.axis_index("tile")
    keys = dest_owners[:, 0] * SLOTS + dest_slots
    table = lax.all_gather(keys, "tile", axis=0)

    product = cycle_products(cycle_blocks, amplitudes, cycle_ints)
    cycle_part = lax.psum_scatter(product, "occ", scatter_dimension=0, tiled=True)

    column, rank = ranks_in_column(keys)
    packed = ladder_terms(
        ladder_sources, ladder_factors, column * TERMS + rank, amplitudes, left_factors,
        right_factors,
    ).reshape(J, NX, TERMS, TW, TW)

    all_ranks = ranks_in_column(table)[1]
    owner = table // SLOTS
    crowd = jnp.sum(
        (owner.reshape(NZ, 8 * TERMS)[:, :, None] % 8 == jnp.arange(8)).astype(jnp.int32), axis=1
    )
    fits = (jnp.max(all_ranks) < SMALL_CAP) & (jnp.max(crowd) <= SMALL_ENTRIES)

    group = (tile // 8) * 8
    here = lax.dynamic_slice_in_dim(table, group, 8, 0).reshape(-1)
    here_rank = lax.dynamic_slice_in_dim(all_ranks, group, 8, 0).reshape(-1)
    number = jnp.arange(8 * TERMS, dtype=jnp.int32)
    valid = (here // SLOTS) % 8 == tile % 8
    target = jnp.where(valid, (here // (SLOTS * 8)) * SLOTS + here % SLOTS, 64)
    order = target * 256 + number
    place = jnp.sum((order[None, :] < order[:, None]).astype(jnp.int32), axis=1)
    hit = place[None, :] == number[:, None]
    source = number // TERMS
    perm_small = jnp.sum(jnp.where(hit, source * SMALL_CAP + here_rank, 0), axis=1)
    perm_full = jnp.sum(jnp.where(hit, source * TERMS + here_rank, 0), axis=1)
    sorted_target = jnp.sum(jnp.where(hit, target, 0), axis=1)
    same = jnp.concatenate(
        [jnp.zeros((1,), jnp.int32), (sorted_target[1:] == sorted_target[:-1]).astype(jnp.int32)]
    )
    goal = jnp.arange(64, dtype=jnp.int32)[:, None]
    end = jnp.maximum(jnp.sum((target[None, :] <= goal).astype(jnp.int32), axis=1) - 1, 0)
    some = jnp.sum((target[None, :] == goal).astype(jnp.int32), axis=1)

    def small():
        return route(
            SMALL_CAP, SMALL_ENTRIES, 0, perm_small[:SMALL_ENTRIES], same[:SMALL_ENTRIES],
            end, some, packed,
        )

    def full():
        return route(TERMS, 8 * TERMS, 1, perm_full, same, end, some, packed)

    ladder = lax.cond(fits, small, full)
    return (
        exchange_ints.astype(jnp.float32) + ladder + cycle_part.astype(jnp.float32)
    ).astype(jnp.bfloat16)


def solution(mesh):
    placed = (
        P("occ", "tile", None, None),
        P("occ", "tile", None, None),
        P("tile", None, None),
        P("tile", None, None),
        P("tile", None),
        P("tile", None),
        P("tile", None),
        P("tile"),
        P("tile"),
        P("tile", "occ", None),
    )
    return jax.shard_map(
        local, mesh=mesh, in_specs=placed, out_specs=P("occ", "tile", None, None), check_vma=False
    )
```

time: 345 us -> 195 us (0.57)
  waiting for transfers between devices: 167 us -> 0.04 us
  Pallas kernels: 0 us -> 142 us
  local copies, waits for them, and re-layouts: 101 us -> 9.4 us
  matrix products: 30.8 us -> 0 us
  starting transfers between devices: 23.5 us -> 0.01 us
  blocking collectives: 0 us -> 20.7 us
    all_to_all x2 -> x0, waiting for transfers between devices: 167 us -> none  [the longest x1 167 us: local(): lax.all_to_all(buffer, 'tile', split_axis=0, concat_axis=0, tiled=True)]
    pallas_call x0 -> x3, Pallas kernels: none -> 142 us  [the longest x1 118 us: route(): pl.pallas_call(functools.partial(route_kernel, cap, entries), out_shape=j...]
    gather x9 -> x0, local copies, waits for them, and re-layouts: 53 us -> none  [the longest x4 37 us: local(): jnp.take(amplitudes, ladder_sources[:, group_start:group_stop], axis=1)]
    dot_general x4 -> x0, matrix products: 30.8 us -> none  [the longest x2 20.2 us: local(): jnp.einsum('gqjad,gqbd->gjab', half_prod, right_tiles, preferred_element_...]
    all_to_all x2 -> x0, starting transfers between devices: 23.5 us -> none  [the longest x1 13 us: local(): lax.all_to_all(labels, 'tile', split_axis=0, concat_axis=0, tiled=True)]
    reshape x2, local copies, waits for them, and re-layouts: 21.6 us -> 0.16 us  [the longest x1 0.08 us: local(): here = lax.dynamic_slice_in_dim(table, group, 8, 0).reshape(-1)]
    unnamed x0 -> x1, blocking collectives: none -> 20.7 us
    all_to_all x3 -> x0, local copies, waits for them, and re-layouts: 11.3 us -> none  [the longest x1 10 us: local(): lax.all_to_all(buffer, 'tile', split_axis=0, concat_axis=0, tiled=True)]
  transfers between devices with their start and end apart: 3 -> 1, of which waited for: 1 -> 0; matrix products, arithmetic and copies ran while one was open for 38% -> 4% of each run, Pallas kernels for 0% -> 71%
where the time goes in v1:
time: 195 us; the launch traced here: 194 us
  Pallas kernels  142 us (73%)
  blocking collectives  20.7 us (11%)
  between operations  15.6 us (8%)
  local copies, waits for them, and re-layouts  9.4 us (5%)
  other arithmetic  6.19 us (3%)
    pallas_call x1, Pallas kernels, route(): pl.pallas_call(functools.partial(route_kernel, cap, entries), out_shape=j...  118 us
    unnamed x1, blocking collectives  20.7 us
    pallas_call x1, Pallas kernels, ladder_terms(): pl.pallas_call(ladder_kernel, out_shape=jax.ShapeDtypeStruct((J, NX * TER...  20.5 us
    unnamed x18, local copies, waits for them, and re-layouts  8.85 us
  transfers between devices with their start and end apart: 1, of which 0 were waited for; matrix products, arithmetic and copies ran while one was open for 4% of the time, Pallas kernels for 71%

profile of v1, /device:TPU:1, one launch (start us, length us, event | category | flops | bytes accessed | tf_op | source)
XLA Modules:
  0.0 194.4 jit_solution(6460376852282110603)
XLA Ops:
  6.5 0.0 reduce-scatter.2.cloned.1.call-start
  6.5 0.0 copy-start
  6.5 1.2 copy-done
  7.8 0.0 copy-start.1
  7.8 1.0 copy-done.1
  8.8 0.0 copy-start.3
  8.8 0.7 copy-done.3
  9.5 3.8 %shard_map.101 = bf16[8,8,128,128]{3,2,1,0:T(8,128)(2,1)} custom-call(s32[8]{0:T(128)S(1)} %copy-done.3, bf16[2,8,128,128]{3,2,1,0:T(8,128)(2,1)S(1)} %copy-done.1, bf16[2,256,1024]{2,1,0:T(8,128)(2,1)S(1)} %copy-done), custom_call_target="tpu_custom_call" | custom-call | flops 536870912 | bytes 4194304 | tf_op jit(solution)/shard_map/pallas_call | solution.py:37
  13.3 0.0 reduce-scatter.2.cloned.1.call-update
  13.3 1.3 dynamic-slice
  15.3 0.8 and_select_fusion
  16.0 20.7 %all-reduce = s32[2048]{0:T(1024)S(1)} all-reduce(s32[2048]{0:T(1024)S(1)} %get-tuple-element.79), channel_id=2, replica_groups=mesh['tile'=64,'occ'=4] {'tile'}, use_global_device_ids=true, to_apply=%add | all-reduce | flops 2048 | bytes 16384
  36.8 0.1 reshape.230
  36.9 0.1 reshape.228
  36.9 0.1 add_select_fusion
  37.0 0.1 copy.19
  37.1 0.2 convert_reduce_fusion
  37.3 0.1 constant_dynamic-slice_fusion.1
  37.4 0.1 copy.21
  37.5 0.1 reshape.227
  37.6 0.8 copy.22.src_ref
  38.3 0.8 copy.23.fac_ref
  39.1 0.6 reduce_max.18
  39.7 0.1 broadcast_in_dim_reshape.3
  39.8 0.2 convert_reduce_fusion.4
  40.0 0.7 reduce_max.19
  42.1 0.2 convert_reduce_fusion.1
  42.3 0.1 select_reduce_fusion.2
  42.4 0.1 slice_compare_fusion
  42.5 0.1 add_convert_fusion.1
  42.6 0.1 convert_reduce_fusion.2
  42.7 0.2 convert_reduce_fusion.5
  43.0 0.0 copy-start.2
  43.0 1.0 copy-done.2
  44.0 0.0 copy-start.4
  44.0 1.0 copy-done.4
  45.1 0.0 copy-start.5
  45.1 1.0 copy-done.5
  46.1 20.5 %shard_map.100 = bf16[2,128,128,128]{3,2,1,0:T(8,128)(2,1)} custom-call(s32[32,8]{1,0:T(8,128)S(1)} %copy.22.src_ref, s32[32,8]{1,0:T(8,128)S(1)} %copy.23.fac_ref, s32[32]{0:T(128)S(1)} %multiply_add_fusion.2.pos_ref, bf16[2,8,128,128]{3,2,1,0:T(8,128)(2,1)S(1)} %copy-done.2, bf16[16,128,128]{2,1,0:T(8,128)(2,1)S(1)} %copy-done.4, ...), custom_call_target="tpu_custom_call" | custom-call | flops 4294967296 | bytes 4194304 | tf_op jit(solution)/shard_map/pallas_call | solution.py:83
  66.6 0.0 copy-start.6
  66.6 118.9 %conditional.1 = (f32[2,8,128,128]{3,2,1,0:T(8,128)S(1)}) conditional(s32[]{:T(128)} %convert_element_type.34, (s32[256]{0:T(256)S(1)}, s32[256]{0:T(256)S(1)}, pred[256,256]{1,0:T(8,128)(4,1)S(1)}, s32[256,256]{1,0:T(8,128)S(1)}, s32[256]{0:T(256)S(1)}, /*index=5*/s32[64]{0:T(128)S(1)}, s32[64]{0:T(128)S(1)}, ...), branch_computations={%region_9.11_spmd, %region_11.13_spmd} | conditional | flops 4325632 | bytes 8722696 | solution.py:344
  66.6 0.7 select_reduce_fusion.perm_ref
  67.3 118.2 %branch_0_fun.1 = f32[2,8,128,128]{3,2,1,0:T(8,128)S(1)} custom-call(s32[256]{0:T(256)} %select_reduce_fusion.perm_ref, s32[256]{0:T(256)S(1)} %get-tuple-element.60.same_ref, s32[64]{0:T(128)S(1)} %get-tuple-element.61.end_ref, s32[64]{0:T(128)S(1)} %get-tuple-element.62.some_ref, bf16[2,4,32,128,128]{4,3,2,1,0:T(8,128)(2,1)} %get-tuple-element.63.p_ref), custom_call_target="tpu_custom_call" | custom-call | flops 4194304 | bytes 8388608 | tf_op jit(solution)/shard_map/cond/branch_0_fun/pallas_call | solution.py:256
  185.5 0.0 reduce-scatter.2.cloned.1.call-done
  185.5 0.0 copy-done.6
  185.5 2.0 %add_convert_fusion = bf16[2,8,128,128]{3,2,1,0:T(8,128)(2,1)} fusion(bf16[2,8,128,128]{3,2,1,0:T(8,128)(2,1)} %reduce-scatter.2.cloned.1.call-done, f32[2,8,128,128]{3,2,1,0:T(8,128)S(1)} %get-tuple-element.80, bf16[2,8,128,128]{3,2,1,0:T(8,128)(2,1)S(1)} %copy-done.6), kind=kLoop, calls=%fused_computation.4 | loop fusion | flops 1310720 | bytes 2621440 | tf_op jit(solution)/shard_map/convert_element_type | solution.py:347
  (11 shorter events, 0.1 us)
Async XLA Ops:
  6.5 179.0 %reduce-scatter.2.cloned.1.call-start = ((), (), s32[]{:S(2)}) async-start(), calls=%async_computation.1 | async-start | bytes 2621440 | tf_op jit(solution)/shard_map/reduce_scatter | solution.py:300
  6.5 1.2 copy-start
  7.8 1.0 copy-start.1
  8.8 0.7 copy-start.3
  43.0 1.0 copy-start.2
  44.0 1.0 copy-start.4
  45.1 1.1 copy-start.5
  66.6 118.9 %copy-start.6 = (bf16[2,8,128,128]{3,2,1,0:T(8,128)(2,1)S(1)}, bf16[2,8,128,128]{3,2,1,0:T(8,128)(2,1)}, u32[]{:S(2)}) copy-start(bf16[2,8,128,128]{3,2,1,0:T(8,128)(2,1)} %param.13) | copy-start | bytes 1572868
Sparse Core Ops, SparseCore 0:
  13.4 36.1 reduce-scatter.1

commit v2 on v1

--- a/solution.py
+++ b/solution.py
@@ -17,33 +17,8 @@
 PARTS = TW // ROWS
 CHUNKS = J * PARTS
 RING = 5
-SMALL_CAP, SMALL_ENTRIES = 14, 80
-
-
-def cycle_kernel(blocks_ref, amp_ref, ints_ref, out_ref):
-    def one(s, _):
-        ints = ints_ref.at[blocks_ref[s]]
-        rows = jnp.concatenate([amp_ref[0, s], amp_ref[1, s]], axis=1)
-        prod = jnp.dot(rows, ints[...], preferred_element_type=jnp.float32)
-        for j in range(8):
-            out_ref[j, s] = prod[:, j * TW : (j + 1) * TW].astype(jnp.bfloat16)
-        return 0
-
-    lax.fori_loop(0, SLOTS, one, 0)
-
-
-def cycle_products(cycle_blocks, amplitudes, cycle_ints):
-    vmem = pl.BlockSpec(memory_space=pltpu.VMEM)
-    return pl.pallas_call(
-        cycle_kernel,
-        out_shape=jax.ShapeDtypeStruct((8, SLOTS, TW, TW), jnp.bfloat16),
-        in_specs=[pl.BlockSpec(memory_space=pltpu.SMEM), vmem, vmem],
-        out_specs=vmem,
-        compiler_params=pltpu.CompilerParams(vmem_limit_bytes=32 * 2**20),
-        cost_estimate=pl.CostEstimate(
-            flops=2 * SLOTS * TW * 256 * 1024, bytes_accessed=4 * 2**20, transcendentals=0
-        ),
-    )(cycle_blocks, amplitudes, cycle_ints)
+CAP = 14
+LANES = 128
 
 
 def ladder_kernel(src_ref, fac_ref, pos_ref, amp_ref, left_ref, right_ref, out_ref, rt, stage, sem):
@@ -98,7 +73,7 @@
 
 
 def route_kernel(
-    cap, entries, perm_ref, same_ref, end_ref, some_ref, p_ref, out_ref,
+    first, cap, entries, perm_ref, same_ref, end_ref, some_ref, p_ref, out_ref,
     recv, stage, sums, zs, zr, xs_sem, fs_sem, lx_sem, rx_sem, zs_sem, zr_sem,
 ):
     t = lax.axis_index("tile")
@@ -121,7 +96,7 @@
     pl.semaphore_wait(barrier, len(partners))
 
     def mine(h, xx):
-        return p_ref.at[h // PARTS, xx, pl.ds(0, cap), pl.ds((h % PARTS) * ROWS, ROWS)]
+        return p_ref.at[h // PARTS, xx, pl.ds(first, cap), pl.ds((h % PARTS) * ROWS, ROWS)]
 
     def send_x(h, d):
         xx = (x + d) % NX
@@ -250,11 +225,11 @@
     lax.fori_loop(0, CHUNKS, drain, 0)
 
 
-def route(cap, entries, collective_id, perm, same, end, some, packed):
+def route(first, cap, entries, collective_id, perm, same, end, some, packed):
     smem = pl.BlockSpec(memory_space=pltpu.SMEM)
     dma = pltpu.SemaphoreType.DMA
     return pl.pallas_call(
-        functools.partial(route_kernel, cap, entries),
+        functools.partial(route_kernel, first, cap, entries),
         out_shape=jax.ShapeDtypeStruct((J, SLOTS, TW, TW), jnp.float32),
         in_specs=[smem, smem, smem, smem, pl.BlockSpec(memory_space=pl.ANY)],
         out_specs=pl.BlockSpec(memory_space=pltpu.VMEM),
@@ -288,63 +263,489 @@
     return column, jnp.sum((alike & earlier).astype(jnp.int32), axis=-1)
 
 
-def local(
-    amplitudes, exchange_ints, left_factors, right_factors, ladder_sources, ladder_factors,
-    dest_owners, dest_slots, cycle_blocks, cycle_ints,
+def row_iota(shape, axis):
+    return lax.broadcasted_iota(jnp.int32, shape, axis)
+
+
+def as_column(row):
+    diagonal = row_iota((LANES, LANES), 0) == row_iota((LANES, LANES), 1)
+    return jnp.sum(jnp.where(diagonal, row, 0), axis=1, keepdims=True)
+
+
+def main_kernel(
+    src_ref, fac_ref, blocks_ref, keys_ref, amp_hbm, exch_hbm, left_hbm, right_hbm, ints_hbm,
+    out_ref, flag_ref,
+    amp_ref, exch_ref, left_ref, right_ref, ints_ref, rt, terms, packed, recv, stage, sums,
+    zs, zr, ysend, yrecv, labels_out, labels_in, flags_out, flags_in, pack_v, plan_v,
+    pack_s, plan_s,
+    in_sem, xs_sem, fs_sem, lx_sem, rx_sem, zs_sem, zr_sem, ys_sem, yr_sem, ls_sem, lr_sem,
+    gs_sem, gr_sem, sm_sem,
+):
+    t = lax.axis_index("tile")
+    y = lax.axis_index("occ")
+    core = t % NC
+    x = (t // NC) % NX
+    z = t // (NC * NX)
+    m = t % (NC * NX)
+
+    def at(zz, xx, cc):
+        return {"tile": (zz * NX + xx) * NC + cc, "occ": y}
+
+    def at_y(d):
+        return {"tile": t, "occ": (y + d) % 4}
+
+    def at_m(d):
+        return {"tile": z * (NX * NC) + (m + d) % (NX * NC), "occ": y}
+
+    def at_z(d):
+        return at((z + d) % NZ, x, core)
+
+    sibling = at(z, x, 1 - core)
+    ups = at_z(1)
+    downs = at_z(NZ - 1)
+
+    loads = [
+        pltpu.make_async_copy(hbm, ref, in_sem.at[n])
+        for n, (hbm, ref) in enumerate(
+            [(right_hbm, right_ref), (left_hbm, left_ref), (amp_hbm, amp_ref),
+             (ints_hbm, ints_ref), (exch_hbm, exch_ref)]
+        )
+    ]
+    for load in loads:
+        load.start()
+
+    barrier = pltpu.get_barrier_semaphore()
+    partners = [at_m(d) for d in range(1, NX * NC)] + [at_z(d) for d in range(1, NZ)]
+    partners = partners + [at_y(d) for d in range(1, 4)]
+    for partner in partners:
+        pl.semaphore_signal(barrier, inc=1, device_id=partner, device_id_type=MESH)
+
+    lane = row_iota((LANES, LANES), 1)
+    line = row_iota((LANES, LANES), 0)
+    keys = keys_ref[...]
+    key_column = as_column(keys)
+    real = line < TERMS
+    column_row = jnp.where(row_iota((1, LANES), 1) < TERMS, (keys // 16) % NX, NX)
+    column = (key_column // 16) % NX
+    rank = jnp.sum(
+        jnp.where((column_row == column) & (lane < line), 1, 0), axis=1, keepdims=True
+    )
+    pack_v[...] = jnp.broadcast_to(
+        jnp.sum(jnp.where(real & (column * TERMS + rank == lane), line, 0), axis=0, keepdims=True),
+        (8, LANES),
+    )
+    label = ((key_column // 8) % NC) * 64 + (key_column // 64) * SLOTS + key_column % SLOTS
+    for xx in range(NX):
+        here = real & (column == xx) & (rank < CAP) & (m * 16 + rank == lane)
+        row = jnp.sum(jnp.where(here, label + 1, 0), axis=0, keepdims=True)
+        labels_out[xx] = jnp.broadcast_to(row, (8, LANES))
+    over = jnp.max(jnp.where(real & (rank >= CAP), 1, 0), axis=0, keepdims=True)
+    labels_out[NX] = jnp.broadcast_to(over, (8, LANES))
+    pack_copy = pltpu.make_async_copy(pack_v, pack_s, sm_sem.at[0])
+    pack_copy.start()
+
+    pl.semaphore_wait(barrier, len(partners))
+
+    def send_label(d, which):
+        if which == 0:
+            part = (((m + d) % (NX * NC)) // NC)
+        else:
+            part = NX
+        return pltpu.make_async_remote_copy(
+            src_ref=labels_out.at[part], dst_ref=labels_in.at[which, m],
+            send_sem=ls_sem.at[which, d], recv_sem=lr_sem.at[which, m],
+            device_id=at_m(d), device_id_type=MESH,
+        )
+
+    def label_from(d, which):
+        source = (m + d) % (NX * NC)
+        return pltpu.make_async_copy(
+            labels_in.at[which, source], labels_in.at[which, source], lr_sem.at[which, source]
+        )
+
+    for d in range(1, NX * NC):
+        for which in range(2):
+            send_label(d, which).start()
+    labels_in[0, m] = labels_out[x]
+    labels_in[1, m] = labels_out[NX]
+
+    loads[0].wait()
+    for f in range(16):
+        rt[f] = right_ref[f].T
+    loads[1].wait()
+    loads[2].wait()
+
+    def one(g, _):
+        halves, rights = [], []
+        for q in range(8):
+            s = src_ref[g, q]
+            f = fac_ref[g, q]
+            amps = jnp.concatenate([amp_ref[0, s], amp_ref[1, s]], axis=1)
+            half = jnp.dot(left_ref[f], amps, preferred_element_type=jnp.float32).astype(
+                jnp.bfloat16
+            )
+            halves.append(jnp.concatenate([half[:, :TW], half[:, TW:]], axis=0))
+            rights.append(rt[f])
+        acc = jnp.dot(
+            jnp.concatenate(halves, axis=1), jnp.concatenate(rights, axis=0),
+            preferred_element_type=jnp.float32,
+        )
+        terms[g] = acc.astype(jnp.bfloat16).reshape(J, TW, TW)
+        return 0
+
+    lax.fori_loop(0, TERMS, one, 0, unroll=4)
+
+    def send_x(h, d):
+        xx = (x + d) % NX
+        return pltpu.make_async_remote_copy(
+            src_ref=packed.at[h, xx], dst_ref=recv.at[h, m],
+            send_sem=xs_sem.at[h, d], recv_sem=rx_sem.at[h, m],
+            device_id=at(z, xx, core), device_id_type=MESH,
+        )
+
+    def send_own(h):
+        return pltpu.make_async_remote_copy(
+            src_ref=packed.at[h, x], dst_ref=recv.at[h, m],
+            send_sem=xs_sem.at[h, 0], recv_sem=rx_sem.at[h, m],
+            device_id=sibling, device_id_type=MESH,
+        )
+
+    def copy_own(h):
+        return pltpu.make_async_copy(packed.at[h, x], recv.at[h, m], lx_sem.at[h])
+
+    def forward(h, d):
+        source = ((x + d) % NX) * NC + core
+        return pltpu.make_async_remote_copy(
+            src_ref=recv.at[h, source], dst_ref=recv.at[h, source],
+            send_sem=fs_sem.at[h, d], recv_sem=rx_sem.at[h, source],
+            device_id=sibling, device_id_type=MESH,
+        )
+
+    def arrived(h, source):
+        return pltpu.make_async_copy(recv.at[h, source], recv.at[h, source], rx_sem.at[h, source])
+
+    def start_x(h):
+        rows = pl.ds((h % PARTS) * ROWS, ROWS)
+        for d in (2, 1, 3, 0):
+            xx = (x + d) % NX
+            for k in range(CAP):
+                packed[h, xx, k] = terms[pack_s[0, xx * TERMS + k], h // PARTS, rows]
+            if d:
+                send_x(h, d).start()
+        send_own(h).start()
+        copy_own(h).start()
+
+    pack_copy.wait()
+    start_x(0)
+    start_x(1)
+
+    got = labels_out[x, 0:1] * 0
+    spill = labels_out[NX, 0:1] * 0
+    for d in range(1, NX * NC):
+        label_from(d, 0).wait()
+        label_from(d, 1).wait()
+    for source in range(NX * NC):
+        got = got + labels_in[0, source, 0:1]
+        spill = spill + labels_in[1, source, 0:1]
+    flags_out[...] = jnp.broadcast_to(spill, (8, LANES))
+
+    def send_flag(d):
+        return pltpu.make_async_remote_copy(
+            src_ref=flags_out, dst_ref=flags_in.at[z],
+            send_sem=gs_sem.at[d], recv_sem=gr_sem.at[z],
+            device_id=at_z(d), device_id_type=MESH,
+        )
+
+    for d in range(1, NZ):
+        send_flag(d).start()
+    flags_in[z] = jnp.broadcast_to(spill, (8, LANES))
+
+    ours = (got > 0) & ((got - 1) // 64 == core)
+    goal_row = jnp.where(ours, (got - 1) % 64, 64)
+    order_row = goal_row * LANES + row_iota((1, LANES), 1)
+    goal = as_column(goal_row)
+    order = goal * LANES + row_iota((LANES, 1), 0)
+    before = order_row < order
+    place = jnp.sum(jnp.where(before, 1, 0), axis=1, keepdims=True)
+    follows = jnp.sum(jnp.where(before & (goal_row == goal), 1, 0), axis=1, keepdims=True)
+    hit = place == lane
+    number = row_iota((LANES, 1), 0)
+    spot = (number // 16) * CAP + jnp.minimum(number % 16, CAP - 1)
+    perm_row = jnp.sum(jnp.where(hit, spot, 0), axis=0, keepdims=True)
+    same_row = jnp.sum(jnp.where(hit, jnp.minimum(follows, 1), 0), axis=0, keepdims=True)
+    end_row = jnp.sum(jnp.where(goal <= lane, 1, 0), axis=0, keepdims=True)
+    end_row = jnp.minimum(jnp.maximum(end_row - 1, 0), LANES - 1)
+    some_row = jnp.sum(jnp.where(goal == lane, 1, 0), axis=0, keepdims=True)
+    pick = row_iota((8, LANES), 0)
+    plan_v[...] = jnp.where(
+        pick == 0, perm_row, jnp.where(pick == 1, same_row, jnp.where(pick == 2, end_row, some_row))
+    )
+    plan_copy = pltpu.make_async_copy(plan_v, plan_s, sm_sem.at[1])
+    plan_copy.start()
+
+    loads[3].wait()
+
+    def cycle(s, _):
+        rows = jnp.concatenate([amp_ref[0, s], amp_ref[1, s]], axis=1)
+        ints = ints_ref[blocks_ref[s]]
+        prod = jnp.dot(rows, ints, preferred_element_type=jnp.float32)
+        for j in range(8):
+            ysend[j, s] = prod[:, j * TW : (j + 1) * TW].astype(jnp.bfloat16)
+        return 0
+
+    lax.fori_loop(0, SLOTS, cycle, 0)
+
+    def send_y(d):
+        return pltpu.make_async_remote_copy(
+            src_ref=ysend.at[pl.ds(((y + d) % 4) * J, J)], dst_ref=yrecv.at[d],
+            send_sem=ys_sem.at[d], recv_sem=yr_sem.at[d],
+            device_id=at_y(d), device_id_type=MESH,
+        )
+
+    for d in range(1, 4):
+        send_y(d).start()
+
+    plan_copy.wait()
+
+    def send_z(h, way, step):
+        if step == 0:
+            part = pl.ds(4 * way, 4)
+        else:
+            part = pl.ds(0, SLOTS)
+        return pltpu.make_async_remote_copy(
+            src_ref=zs.at[h, way, step, part], dst_ref=zr.at[h, way, step, part],
+            send_sem=zs_sem.at[h, way, step], recv_sem=zr_sem.at[h, way, step],
+            device_id=ups if way == 0 else downs, device_id_type=MESH,
+        )
+
+    def own(h, zz, s):
+        goal = zz * SLOTS + s
+        value = sums[h % RING, plan_s[2, goal]]
+        return jnp.where(plan_s[3, goal] != 0, value, 0.0)
+
+    def z_step(h, step):
+        for way in range(2):
+            if step > 0:
+                send_z(h, way, step - 1).wait_recv()
+            zz = (z + 4 - step) % NZ if way == 0 else (z + 4 + step) % NZ
+            for s in range(4 * way, 4 * way + 4) if step == 0 else range(SLOTS):
+                value = own(h, zz, s)
+                if step > 1 or (step == 1 and s // 4 == way):
+                    value = value + zr[h, way, step - 1, s].astype(jnp.float32)
+                zs[h, way, step, s] = value.astype(jnp.bfloat16)
+            send_z(h, way, step).start()
+
+    def finish(h):
+        rows = pl.ds((h % PARTS) * ROWS, ROWS)
+        for way in range(2):
+            send_z(h, way, 3).wait_recv()
+        for s in range(SLOTS):
+            total = own(h, z, s) + zr[h, 0, 3, s].astype(jnp.float32)
+            total = total + zr[h, 1, 3, s].astype(jnp.float32)
+            out_ref[h // PARTS, s, rows] = total
+
+    def collect(h):
+        for d in range(1, NX):
+            arrived(h, ((x + d) % NX) * NC + core).wait()
+            forward(h, d).start()
+        copy_own(h).wait()
+        for d in range(NX):
+            arrived(h, ((x + d) % NX) * NC + 1 - core).wait()
+        for source in range(NX * NC):
+            stage[source * CAP : (source + 1) * CAP] = recv[h, source]
+
+        def entry(e, total):
+            value = stage[plan_s[0, e]].astype(jnp.float32)
+            total = value + jnp.where(plan_s[1, e] != 0, total, 0.0)
+            sums[h % RING, e] = total
+            return total
+
+        lax.fori_loop(0, NX * NC * CAP, entry, jnp.zeros((ROWS, TW), jnp.float32), unroll=4)
+
+    def turn(i, _):
+        @pl.when((i >= 1) & (i + 1 < CHUNKS))
+        def _():
+            start_x(i + 1)
+
+        @pl.when(i < CHUNKS)
+        def _():
+            collect(i)
+            z_step(i, 0)
+
+        for step in range(1, 4):
+            @pl.when((i >= step) & (i - step < CHUNKS))
+            def _(step=step):
+                z_step(i - step, step)
+
+        @pl.when(i >= 4)
+        def _():
+            finish(i - 4)
+
+        return 0
+
+    lax.fori_loop(0, CHUNKS + 4, turn, 0)
+
+    loads[4].wait()
+    for d in range(1, 4):
+        send_y(d).wait_recv()
+
+    def add(s, _):
+        for j in range(J):
+            total = out_ref[j, s] + exch_ref[j, s].astype(jnp.float32)
+            total = total + ysend[y * J + j, s].astype(jnp.float32)
+            for d in range(1, 4):
+                total = total + yrecv[d, j, s].astype(jnp.float32)
+            out_ref[j, s] = total
+        return 0
+
+    lax.fori_loop(0, SLOTS, add, 0)
+
+    flags = flags_in[z]
+    for d in range(1, NZ):
+        source = (z + d) % NZ
+        pltpu.make_async_copy(flags_in.at[source], flags_in.at[source], gr_sem.at[source]).wait()
+        flags = flags + flags_in[source]
+    flag_ref[...] = flags
+
+    for d in range(1, NX * NC):
+        for which in range(2):
+            send_label(d, which).wait_send()
+    for d in range(1, NZ):
+        send_flag(d).wait_send()
+    for d in range(1, 4):
+        send_y(d).wait_send()
+
+    def drain(h, _):
+        for d in range(1, NX):
+            send_x(h, d).wait_send()
+            forward(h, d).wait_send()
+        send_own(h).wait_send()
+        for way in range(2):
+            for step in range(4):
+                send_z(h, way, step).wait_send()
+        return 0
+
+    lax.fori_loop(0, CHUNKS, drain, 0)
+
+
+def main_call(sources, factors, blocks, keys, amplitudes, exchange, left, right, ints):
+    smem = pl.BlockSpec(memory_space=pltpu.SMEM)
+    vmem = pl.BlockSpec(memory_space=pltpu.VMEM)
+    hbm = pl.BlockSpec(memory_space=pl.ANY)
+    dma = pltpu.SemaphoreType.DMA
+    entries = NX * NC * CAP
+    block = (J, SLOTS, TW, TW)
+    return pl.pallas_call(
+        main_kernel,
+        out_shape=[
+            jax.ShapeDtypeStruct(block, jnp.float32),
+            jax.ShapeDtypeStruct((8, LANES), jnp.int32),
+        ],
+        in_specs=[smem, smem, smem, vmem, hbm, hbm, hbm, hbm, hbm],
+        out_specs=[vmem, vmem],
+        scratch_shapes=[
+            pltpu.VMEM(block, jnp.bfloat16),
+            pltpu.VMEM(block, jnp.bfloat16),
+            pltpu.VMEM((16, TW, TW), jnp.bfloat16),
+            pltpu.VMEM((16, TW, TW), jnp.bfloat16),
+            pltpu.VMEM((2, 2 * TW, 8 * TW), jnp.bfloat16),
+            pltpu.VMEM((16, TW, TW), jnp.bfloat16),
+            pltpu.VMEM((TERMS, J, TW, TW), jnp.bfloat16),
+            pltpu.VMEM((CHUNKS, NX, CAP, ROWS, TW), jnp.bfloat16),
+            pltpu.VMEM((CHUNKS, NX * NC, CAP, ROWS, TW), jnp.bfloat16),
+            pltpu.VMEM((entries, ROWS, TW), jnp.bfloat16),
+            pltpu.VMEM((RING, LANES, ROWS, TW), jnp.float32),
+            pltpu.VMEM((CHUNKS, 2, 4, SLOTS, ROWS, TW), jnp.bfloat16),
+            pltpu.VMEM((CHUNKS, 2, 4, SLOTS, ROWS, TW), jnp.bfloat16),
+            pltpu.VMEM((8, SLOTS, TW, TW), jnp.bfloat16),
+            pltpu.VMEM((4,) + block, jnp.bfloat16),
+            pltpu.VMEM((NX + 1, 8, LANES), jnp.int32),
+            pltpu.VMEM((2, NX * NC, 8, LANES), jnp.int32),
+            pltpu.VMEM((8, LANES), jnp.int32),
+            pltpu.VMEM((NZ, 8, LANES), jnp.int32),
+            pltpu.VMEM((8, LANES), jnp.int32),
+            pltpu.VMEM((8, LANES), jnp.int32),
+            pltpu.SMEM((8, LANES), jnp.int32),
+            pltpu.SMEM((8, LANES), jnp.int32),
+            dma((5,)),
+            dma((CHUNKS, NX)),
+            dma((CHUNKS, NX)),
+            dma((CHUNKS,)),
+            dma((CHUNKS, NX * NC)),
+            dma((CHUNKS, 2, 4)),
+            dma((CHUNKS, 2, 4)),
+            dma((4,)),
+            dma((4,)),
+            dma((2, NX * NC)),
+            dma((2, NX * NC)),
+            dma((NZ,)),
+            dma((NZ,)),
+            dma((2,)),
+        ],
+        compiler_params=pltpu.CompilerParams(
+            collective_id=0, has_side_effects=True, vmem_limit_bytes=58 * 2**20
+        ),
+        cost_estimate=pl.CostEstimate(
+            flops=2 * 1024 * TW**3, bytes_accessed=8 * 2**20, transcendentals=0
+        ),
+    )(sources, factors, blocks, keys, amplitudes, exchange, left, right, ints)
+
+
+def spilled(
+    amplitudes, left_factors, right_factors, ladder_sources, ladder_factors, keys
 ):
     tile = lax.axis_index("tile")
-    keys = dest_owners[:, 0] * SLOTS + dest_slots
     table = lax.all_gather(keys, "tile", axis=0)
-
-    product = cycle_products(cycle_blocks, amplitudes, cycle_ints)
-    cycle_part = lax.psum_scatter(product, "occ", scatter_dimension=0, tiled=True)
-
     column, rank = ranks_in_column(keys)
     packed = ladder_terms(
         ladder_sources, ladder_factors, column * TERMS + rank, amplitudes, left_factors,
         right_factors,
     ).reshape(J, NX, TERMS, TW, TW)
-
+    width = TERMS - CAP
     all_ranks = ranks_in_column(table)[1]
-    owner = table // SLOTS
-    crowd = jnp.sum(
-        (owner.reshape(NZ, 8 * TERMS)[:, :, None] % 8 == jnp.arange(8)).astype(jnp.int32), axis=1
-    )
-    fits = (jnp.max(all_ranks) < SMALL_CAP) & (jnp.max(crowd) <= SMALL_ENTRIES)
-
     group = (tile // 8) * 8
     here = lax.dynamic_slice_in_dim(table, group, 8, 0).reshape(-1)
     here_rank = lax.dynamic_slice_in_dim(all_ranks, group, 8, 0).reshape(-1)
     number = jnp.arange(8 * TERMS, dtype=jnp.int32)
-    valid = (here // SLOTS) % 8 == tile % 8
+    valid = ((here // SLOTS) % 8 == tile % 8) & (here_rank >= CAP)
     target = jnp.where(valid, (here // (SLOTS * 8)) * SLOTS + here % SLOTS, 64)
     order = target * 256 + number
     place = jnp.sum((order[None, :] < order[:, None]).astype(jnp.int32), axis=1)
     hit = place[None, :] == number[:, None]
-    source = number // TERMS
-    perm_small = jnp.sum(jnp.where(hit, source * SMALL_CAP + here_rank, 0), axis=1)
-    perm_full = jnp.sum(jnp.where(hit, source * TERMS + here_rank, 0), axis=1)
-    sorted_target = jnp.sum(jnp.where(hit, target, 0), axis=1)
+    spot = (number // TERMS) * width + jnp.maximum(here_rank - CAP, 0)
+    perm = jnp.sum(jnp.where(hit, spot[None, :], 0), axis=1)
+    sorted_target = jnp.sum(jnp.where(hit, target[None, :], 0), axis=1)
     same = jnp.concatenate(
         [jnp.zeros((1,), jnp.int32), (sorted_target[1:] == sorted_target[:-1]).astype(jnp.int32)]
     )
     goal = jnp.arange(64, dtype=jnp.int32)[:, None]
     end = jnp.maximum(jnp.sum((target[None, :] <= goal).astype(jnp.int32), axis=1) - 1, 0)
     some = jnp.sum((target[None, :] == goal).astype(jnp.int32), axis=1)
-
-    def small():
-        return route(
-            SMALL_CAP, SMALL_ENTRIES, 0, perm_small[:SMALL_ENTRIES], same[:SMALL_ENTRIES],
-            end, some, packed,
-        )
-
-    def full():
-        return route(TERMS, 8 * TERMS, 1, perm_full, same, end, some, packed)
-
-    ladder = lax.cond(fits, small, full)
-    return (
-        exchange_ints.astype(jnp.float32) + ladder + cycle_part.astype(jnp.float32)
-    ).astype(jnp.bfloat16)
+    entries = 8 * width
+    return route(CAP, width, entries, 1, perm[:entries], same[:entries], end, some, packed)
+
+
+def local(
+    amplitudes, exchange_ints, left_factors, right_factors, ladder_sources, ladder_factors,
+    dest_owners, dest_slots, cycle_blocks, cycle_ints,
+):
+    keys = dest_owners[:, 0] * SLOTS + dest_slots
+    row = jnp.pad(keys, (0, LANES - TERMS))[None, :]
+    total, flags = main_call(
+        ladder_sources, ladder_factors, cycle_blocks, row, amplitudes, exchange_ints,
+        left_factors, right_factors, cycle_ints,
+    )
+
+    def whole():
+        return total.astype(jnp.bfloat16)
+
+    def more():
+        rest = spilled(
+            amplitudes, left_factors, right_factors, ladder_sources, ladder_factors, keys
+        )
+        return (total + rest).astype(jnp.bfloat16)
+
+    return lax.cond(jnp.max(flags) > 0, more, whole)
 
 
 def solution(mesh):

time: 195 us -> 95.1 us (0.49)
  Pallas kernels: 142 us -> 87.7 us
  blocking collectives: 20.7 us -> 0 us
  between operations: 15.6 us -> 0.73 us
  local copies, waits for them, and re-layouts: 9.4 us -> 3.28 us
  other arithmetic: 6.19 us -> 2.99 us
    pallas_call x3 -> x1, Pallas kernels: 142 us -> 87.7 us  [main_call(): pl.pallas_call(main_kernel, out_shape=[jax.ShapeDtypeStruct(block, jnp.fl...]
    unnamed x1 -> x0, blocking collectives: 20.7 us -> none
    unnamed x18 -> x12, local copies, waits for them, and re-layouts: 8.85 us -> 2.74 us
  transfers between devices with their start and end apart: 1 -> 0, of which waited for: 0 -> 0; matrix products, arithmetic and copies ran while one was open for 4% -> 0% of each run, Pallas kernels for 71% -> 0%
where the time goes in v2:
time: 95.1 us; the launch traced here: 94.7 us
  Pallas kernels  87.7 us (92%)
  local copies, waits for them, and re-layouts  3.28 us (3%)
  other arithmetic  2.99 us (3%)
    pallas_call x1, Pallas kernels, main_call(): pl.pallas_call(main_kernel, out_shape=[jax.ShapeDtypeStruct(block, jnp.fl...  87.7 us
    unnamed x12, local copies, waits for them, and re-layouts  2.74 us

profile of v2, /device:TPU:1, one launch (start us, length us, event | category | flops | bytes accessed | tf_op | source)
XLA Modules:
  0.0 94.7 jit_solution(2063382150919954690)
XLA Ops:
  0.0 0.0 copy-start.2
  0.0 0.0 copy-start.1
  0.0 0.0 copy-start.5
  0.0 0.0 copy-start.4
  0.0 0.0 copy-start.3
  0.0 0.8 bitcast_add_fusion
  0.8 0.5 pad_bitcast_fusion.keys_ref
  1.4 1.4 %copy.38.src_ref = s32[32,8]{1,0:T(8,128)} copy(s32[32,8]{0,1:T(8,128)} %param.16) | data formatting | bytes 2048 | tf_op args[4]
  2.7 1.4 %copy.39.fac_ref = s32[32,8]{1,0:T(8,128)} copy(s32[32,8]{0,1:T(8,128)} %param.17) | data formatting | bytes 2048 | tf_op args[5]
  4.1 87.7 %shard_map.102 = (f32[2,8,128,128]{3,2,1,0:T(8,128)S(1)}, s32[8,128]{1,0:T(8,128)}) custom-call(s32[32,8]{1,0:T(8,128)} %copy.38.src_ref, s32[32,8]{1,0:T(8,128)} %copy.39.fac_ref, s32[8]{0:T(128)} %blocks_ref.1, s32[1,128]{1,0:T(1,128)} %pad_bitcast_fusion.keys_ref, bf16[2,8,128,128]{3,2,1,0:T(8,128)(2,1)} %amp_hbm.1, bf16[2,8,128,128]{3,2,1,0:T(8,128)(2,1)} %exch_hbm.1, ...), custom_call_target="tpu_custom_call" | custom-call | flops 4294967296 | bytes 8388608 | tf_op jit(solution)/shard_map/pallas_call | solution.py:638
  91.8 1.3 %reduce_max.9 = s32[]{:T(128)} reduce(s32[8,128]{1,0:T(8,128)} %get-tuple-element.40, s32[]{:T(128)} %constant.149.clone.1), dimensions={0,1}, to_apply=%region_0.1 | reduce | flops 1023 | bytes 4104 | tf_op jit(solution)/shard_map/reduce_max | solution.py:748
  93.8 0.0 copy-done.2
  93.8 0.0 copy-done.1
  93.8 0.0 copy-done.5
  93.8 0.0 copy-done.4
  93.8 0.0 copy-done.3
  93.8 0.9 convert_element_type.32
  (1 shorter events, 0.0 us)
Async XLA Ops:
  0.0 93.8 %copy-start.2 = (s32[32,8]{0,1:T(8,128)S(1)}, s32[32,8]{0,1:T(8,128)}, u32[]{:S(2)}) copy-start(s32[32,8]{0,1:T(8,128)} %param.17) | copy-start | bytes 3076
  0.0 93.8 %copy-start.1 = (s32[32,8]{0,1:T(8,128)S(1)}, s32[32,8]{0,1:T(8,128)}, u32[]{:S(2)}) copy-start(s32[32,8]{0,1:T(8,128)} %param.16) | copy-start | bytes 3076
  0.0 93.8 %copy-start.5 = (bf16[16,128,128]{2,1,0:T(8,128)(2,1)S(1)}, bf16[16,128,128]{2,1,0:T(8,128)(2,1)}, u32[]{:S(2)}) copy-start(bf16[16,128,128]{2,1,0:T(8,128)(2,1)} %right_hbm.1) | copy-start | bytes 1572868
  0.0 93.8 %copy-start.4 = (bf16[16,128,128]{2,1,0:T(8,128)(2,1)S(1)}, bf16[16,128,128]{2,1,0:T(8,128)(2,1)}, u32[]{:S(2)}) copy-start(bf16[16,128,128]{2,1,0:T(8,128)(2,1)} %left_hbm.1) | copy-start | bytes 1572868
  0.0 93.8 %copy-start.3 = (bf16[2,8,128,128]{3,2,1,0:T(8,128)(2,1)S(1)}, bf16[2,8,128,128]{3,2,1,0:T(8,128)(2,1)}, u32[]{:S(2)}) copy-start(bf16[2,8,128,128]{3,2,1,0:T(8,128)(2,1)} %amp_hbm.1) | copy-start | bytes 1572868

commit v3 on v2

--- a/solution.py
+++ b/solution.py
@@ -19,6 +19,11 @@
 RING = 5
 CAP = 14
 LANES = 128
+LAG = 1
+HALF = 16
+QUARTERS = TW // 2 // HALF
+STEPS = J * QUARTERS
+GOALS = NC * SLOTS
 
 
 def ladder_kernel(src_ref, fac_ref, pos_ref, amp_ref, left_ref, right_ref, out_ref, rt, stage, sem):
@@ -273,13 +278,13 @@
 
 
 def main_kernel(
-    src_ref, fac_ref, blocks_ref, keys_ref, amp_hbm, exch_hbm, left_hbm, right_hbm, ints_hbm,
+    blocks_ref, owners_ref, slots_ref, src_hbm, fac_hbm, amp_hbm, exch_hbm, left_hbm, right_hbm, ints_hbm,
     out_ref, flag_ref,
-    amp_ref, exch_ref, left_ref, right_ref, ints_ref, rt, terms, packed, recv, stage, sums,
-    zs, zr, ysend, yrecv, labels_out, labels_in, flags_out, flags_in, pack_v, plan_v,
-    pack_s, plan_s,
-    in_sem, xs_sem, fs_sem, lx_sem, rx_sem, zs_sem, zr_sem, ys_sem, yr_sem, ls_sem, lr_sem,
-    gs_sem, gr_sem, sm_sem,
+    src_ref, fac_ref, keys_v, amp_ref, exch_ref, left_ref, right_ref, ints_ref, rt, terms, packed, recv, stage, sums,
+    zs, zr, ysend, yrecv, fsend, frecv, labels_out, labels_in, flags_out, flags_in,
+    pack_v, plan_v, pack_s, plan_s, flag_s,
+    in_sem, xs_sem, lx_sem, rx_sem, zs_sem, zr_sem, ys_sem, yr_sem, ls_sem, lr_sem,
+    gs_sem, gr_sem, sm_sem, es_sem, er_sem,
 ):
     t = lax.axis_index("tile")
     y = lax.axis_index("occ")
@@ -308,7 +313,7 @@
         pltpu.make_async_copy(hbm, ref, in_sem.at[n])
         for n, (hbm, ref) in enumerate(
             [(right_hbm, right_ref), (left_hbm, left_ref), (amp_hbm, amp_ref),
-             (ints_hbm, ints_ref), (exch_hbm, exch_ref)]
+             (ints_hbm, ints_ref), (exch_hbm, exch_ref), (src_hbm, src_ref), (fac_hbm, fac_ref)]
         )
     ]
     for load in loads:
@@ -322,7 +327,9 @@
 
     lane = row_iota((LANES, LANES), 1)
     line = row_iota((LANES, LANES), 0)
-    keys = keys_ref[...]
+    keys_v[...] = jnp.zeros((8, LANES), jnp.int32)
+    keys_v[0:1, 0:TERMS] = owners_ref[...] * SLOTS + slots_ref[...]
+    keys = keys_v[0:1]
     key_column = as_column(keys)
     real = line < TERMS
     column_row = jnp.where(row_iota((1, LANES), 1) < TERMS, (keys // 16) % NX, NX)
@@ -375,68 +382,64 @@
     loads[1].wait()
     loads[2].wait()
 
-    def one(g, _):
+    loads[5].wait()
+    loads[6].wait()
+
+    def one(g, j):
         halves, rights = [], []
         for q in range(8):
-            s = src_ref[g, q]
-            f = fac_ref[g, q]
-            amps = jnp.concatenate([amp_ref[0, s], amp_ref[1, s]], axis=1)
-            half = jnp.dot(left_ref[f], amps, preferred_element_type=jnp.float32).astype(
-                jnp.bfloat16
+            f = fac_ref[q, g]
+            half = jnp.dot(
+                left_ref[f], amp_ref[j, src_ref[q, g]], preferred_element_type=jnp.float32
             )
-            halves.append(jnp.concatenate([half[:, :TW], half[:, TW:]], axis=0))
+            halves.append(half.astype(jnp.bfloat16))
             rights.append(rt[f])
         acc = jnp.dot(
             jnp.concatenate(halves, axis=1), jnp.concatenate(rights, axis=0),
             preferred_element_type=jnp.float32,
         )
-        terms[g] = acc.astype(jnp.bfloat16).reshape(J, TW, TW)
-        return 0
+        terms[j, g] = acc.astype(jnp.bfloat16)
+        return j
 
     lax.fori_loop(0, TERMS, one, 0, unroll=4)
 
-    def send_x(h, d):
-        xx = (x + d) % NX
-        return pltpu.make_async_remote_copy(
-            src_ref=packed.at[h, xx], dst_ref=recv.at[h, m],
-            send_sem=xs_sem.at[h, d], recv_sem=rx_sem.at[h, m],
-            device_id=at(z, xx, core), device_id_type=MESH,
+    def send_x(h, d, cc):
+        to = at(z, (x + d) % NX, cc)
+        return pltpu.make_async_remote_copy(
+            src_ref=packed.at[h, (x + d) % NX, cc], dst_ref=recv.at[h, m],
+            send_sem=xs_sem.at[h, d, cc], recv_sem=rx_sem.at[h, m],
+            device_id=to, device_id_type=MESH,
         )
 
     def send_own(h):
         return pltpu.make_async_remote_copy(
-            src_ref=packed.at[h, x], dst_ref=recv.at[h, m],
-            send_sem=xs_sem.at[h, 0], recv_sem=rx_sem.at[h, m],
+            src_ref=packed.at[h, x, 1 - core], dst_ref=recv.at[h, m],
+            send_sem=xs_sem.at[h, 0, 0], recv_sem=rx_sem.at[h, m],
             device_id=sibling, device_id_type=MESH,
         )
 
     def copy_own(h):
-        return pltpu.make_async_copy(packed.at[h, x], recv.at[h, m], lx_sem.at[h])
-
-    def forward(h, d):
-        source = ((x + d) % NX) * NC + core
-        return pltpu.make_async_remote_copy(
-            src_ref=recv.at[h, source], dst_ref=recv.at[h, source],
-            send_sem=fs_sem.at[h, d], recv_sem=rx_sem.at[h, source],
-            device_id=sibling, device_id_type=MESH,
-        )
+        return pltpu.make_async_copy(packed.at[h, x, core], recv.at[h, m], lx_sem.at[h])
 
     def arrived(h, source):
         return pltpu.make_async_copy(recv.at[h, source], recv.at[h, source], rx_sem.at[h, source])
 
     def start_x(h):
-        rows = pl.ds((h % PARTS) * ROWS, ROWS)
         for d in (2, 1, 3, 0):
             xx = (x + d) % NX
-            for k in range(CAP):
-                packed[h, xx, k] = terms[pack_s[0, xx * TERMS + k], h // PARTS, rows]
+            for cc in range(NC):
+                rows = pl.ds(cc * (TW // 2) + (h % QUARTERS) * HALF, HALF)
+                for k in range(CAP):
+                    packed[h, xx, cc, k] = terms[h // QUARTERS, pack_s[0, xx * TERMS + k], rows]
             if d:
-                send_x(h, d).start()
+                for cc in range(NC):
+                    send_x(h, d, cc).start()
         send_own(h).start()
         copy_own(h).start()
 
     pack_copy.wait()
     start_x(0)
+    lax.fori_loop(0, TERMS, one, 1, unroll=4)
     start_x(1)
 
     got = labels_out[x, 0:1] * 0
@@ -460,8 +463,7 @@
         send_flag(d).start()
     flags_in[z] = jnp.broadcast_to(spill, (8, LANES))
 
-    ours = (got > 0) & ((got - 1) // 64 == core)
-    goal_row = jnp.where(ours, (got - 1) % 64, 64)
+    goal_row = jnp.where(got > 0, got - 1, LANES)
     order_row = goal_row * LANES + row_iota((1, LANES), 1)
     goal = as_column(goal_row)
     order = goal * LANES + row_iota((LANES, 1), 0)
@@ -474,7 +476,7 @@
     perm_row = jnp.sum(jnp.where(hit, spot, 0), axis=0, keepdims=True)
     same_row = jnp.sum(jnp.where(hit, jnp.minimum(follows, 1), 0), axis=0, keepdims=True)
     end_row = jnp.sum(jnp.where(goal <= lane, 1, 0), axis=0, keepdims=True)
-    end_row = jnp.minimum(jnp.maximum(end_row - 1, 0), LANES - 1)
+    end_row = jnp.minimum(jnp.maximum(end_row - 1, 0), NX * NC * CAP - 1)
     some_row = jnp.sum(jnp.where(goal == lane, 1, 0), axis=0, keepdims=True)
     pick = row_iota((8, LANES), 0)
     plan_v[...] = jnp.where(
@@ -483,8 +485,6 @@
     plan_copy = pltpu.make_async_copy(plan_v, plan_s, sm_sem.at[1])
     plan_copy.start()
 
-    loads[3].wait()
-
     def cycle(s, _):
         rows = jnp.concatenate([amp_ref[0, s], amp_ref[1, s]], axis=1)
         ints = ints_ref[blocks_ref[s]]
@@ -493,8 +493,6 @@
             ysend[j, s] = prod[:, j * TW : (j + 1) * TW].astype(jnp.bfloat16)
         return 0
 
-    lax.fori_loop(0, SLOTS, cycle, 0)
-
     def send_y(d):
         return pltpu.make_async_remote_copy(
             src_ref=ysend.at[pl.ds(((y + d) % 4) * J, J)], dst_ref=yrecv.at[d],
@@ -502,25 +500,22 @@
             device_id=at_y(d), device_id_type=MESH,
         )
 
-    for d in range(1, 4):
-        send_y(d).start()
-
     plan_copy.wait()
 
     def send_z(h, way, step):
         if step == 0:
-            part = pl.ds(4 * way, 4)
+            part = pl.ds(SLOTS * way, SLOTS)
         else:
-            part = pl.ds(0, SLOTS)
+            part = pl.ds(0, GOALS)
         return pltpu.make_async_remote_copy(
             src_ref=zs.at[h, way, step, part], dst_ref=zr.at[h, way, step, part],
             send_sem=zs_sem.at[h, way, step], recv_sem=zr_sem.at[h, way, step],
             device_id=ups if way == 0 else downs, device_id_type=MESH,
         )
 
-    def own(h, zz, s):
-        goal = zz * SLOTS + s
-        value = sums[h % RING, plan_s[2, goal]]
+    def own(h, zz, n):
+        goal = (n // SLOTS) * 64 + zz * SLOTS + n % SLOTS
+        value = sums[h, plan_s[2, goal]]
         return jnp.where(plan_s[3, goal] != 0, value, 0.0)
 
     def z_step(h, step):
@@ -528,62 +523,94 @@
             if step > 0:
                 send_z(h, way, step - 1).wait_recv()
             zz = (z + 4 - step) % NZ if way == 0 else (z + 4 + step) % NZ
-            for s in range(4 * way, 4 * way + 4) if step == 0 else range(SLOTS):
-                value = own(h, zz, s)
-                if step > 1 or (step == 1 and s // 4 == way):
-                    value = value + zr[h, way, step - 1, s].astype(jnp.float32)
-                zs[h, way, step, s] = value.astype(jnp.bfloat16)
+            for n in range(SLOTS * way, SLOTS * way + SLOTS) if step == 0 else range(GOALS):
+                value = own(h, zz, n)
+                if step > 1 or (step == 1 and n // SLOTS == way):
+                    value = value + zr[h, way, step - 1, n].astype(jnp.float32)
+                zs[h, way, step, n] = value.astype(jnp.bfloat16)
             send_z(h, way, step).start()
 
+    def send_end(h):
+        return pltpu.make_async_remote_copy(
+            src_ref=fsend.at[h], dst_ref=frecv.at[h], send_sem=es_sem.at[h],
+            recv_sem=er_sem.at[h], device_id=sibling, device_id_type=MESH,
+        )
+
     def finish(h):
-        rows = pl.ds((h % PARTS) * ROWS, ROWS)
         for way in range(2):
             send_z(h, way, 3).wait_recv()
+
+        def total(cc, s):
+            n = cc * SLOTS + s
+            value = own(h, z, n) + zr[h, 0, 3, n].astype(jnp.float32)
+            return value + zr[h, 1, 3, n].astype(jnp.float32)
+
         for s in range(SLOTS):
-            total = own(h, z, s) + zr[h, 0, 3, s].astype(jnp.float32)
-            total = total + zr[h, 1, 3, s].astype(jnp.float32)
-            out_ref[h // PARTS, s, rows] = total
+            fsend[h, s] = total(1 - core, s)
+        send_end(h).start()
+        rows = pl.ds(core * (TW // 2) + (h % QUARTERS) * HALF, HALF)
+        for s in range(SLOTS):
+            out_ref[h // QUARTERS, s, rows] = total(core, s)
 
     def collect(h):
-        for d in range(1, NX):
-            arrived(h, ((x + d) % NX) * NC + core).wait()
-            forward(h, d).start()
         copy_own(h).wait()
-        for d in range(NX):
-            arrived(h, ((x + d) % NX) * NC + 1 - core).wait()
+        for d in range(1, NX * NC):
+            arrived(h, (m + d) % (NX * NC)).wait()
         for source in range(NX * NC):
             stage[source * CAP : (source + 1) * CAP] = recv[h, source]
 
         def entry(e, total):
             value = stage[plan_s[0, e]].astype(jnp.float32)
             total = value + jnp.where(plan_s[1, e] != 0, total, 0.0)
-            sums[h % RING, e] = total
+            sums[h, e] = total
             return total
 
-        lax.fori_loop(0, NX * NC * CAP, entry, jnp.zeros((ROWS, TW), jnp.float32), unroll=4)
+        lax.fori_loop(0, NX * NC * CAP, entry, jnp.zeros((HALF, TW), jnp.float32), unroll=8)
 
     def turn(i, _):
-        @pl.when((i >= 1) & (i + 1 < CHUNKS))
+        @pl.when(i + 2 < STEPS)
         def _():
-            start_x(i + 1)
-
-        @pl.when(i < CHUNKS)
+            start_x(i + 2)
+
+        @pl.when(i < STEPS)
         def _():
             collect(i)
             z_step(i, 0)
 
         for step in range(1, 4):
-            @pl.when((i >= step) & (i - step < CHUNKS))
+            @pl.when((i >= LAG * step) & (i - LAG * step < STEPS))
             def _(step=step):
-                z_step(i - step, step)
-
-        @pl.when(i >= 4)
+                z_step(i - LAG * step, step)
+
+        @pl.when(i < 2)
         def _():
-            finish(i - 4)
+            @pl.when(i == 0)
+            def _():
+                loads[3].wait()
+
+            lax.fori_loop(i * 4, i * 4 + 4, cycle, 0)
+
+            @pl.when(i == 1)
+            def _():
+                for d in range(1, 4):
+                    send_y(d).start()
+
+        @pl.when(i >= LAG * 4)
+        def _():
+            finish(i - LAG * 4)
 
         return 0
 
-    lax.fori_loop(0, CHUNKS + 4, turn, 0)
+    lax.fori_loop(0, STEPS + LAG * 4, turn, 0)
+
+    def ending(h, _):
+        send_end(h).wait_recv()
+        rows = pl.ds((1 - core) * (TW // 2) + (h % QUARTERS) * HALF, HALF)
+        for s in range(SLOTS):
+            out_ref[h // QUARTERS, s, rows] = frecv[h, s]
+        return 0
+
+    lax.fori_loop(0, STEPS, ending, 0)
 
     loads[4].wait()
     for d in range(1, 4):
@@ -605,7 +632,9 @@
         source = (z + d) % NZ
         pltpu.make_async_copy(flags_in.at[source], flags_in.at[source], gr_sem.at[source]).wait()
         flags = flags + flags_in[source]
-    flag_ref[...] = flags
+    pack_v[...] = jnp.broadcast_to(jnp.max(flags, axis=1, keepdims=True), (8, LANES))
+    flag_copy = pltpu.make_async_copy(pack_v, flag_s, sm_sem.at[2])
+    flag_copy.start()
 
     for d in range(1, NX * NC):
         for which in range(2):
@@ -617,18 +646,21 @@
 
     def drain(h, _):
         for d in range(1, NX):
-            send_x(h, d).wait_send()
-            forward(h, d).wait_send()
+            for cc in range(NC):
+                send_x(h, d, cc).wait_send()
         send_own(h).wait_send()
+        send_end(h).wait_send()
         for way in range(2):
             for step in range(4):
                 send_z(h, way, step).wait_send()
         return 0
 
-    lax.fori_loop(0, CHUNKS, drain, 0)
-
-
-def main_call(sources, factors, blocks, keys, amplitudes, exchange, left, right, ints):
+    lax.fori_loop(0, STEPS, drain, 0)
+    flag_copy.wait()
+    flag_ref[0] = flag_s[0, 0]
+
+
+def main_call(sources, factors, blocks, owners, slots, amplitudes, exchange, left, right, ints):
     smem = pl.BlockSpec(memory_space=pltpu.SMEM)
     vmem = pl.BlockSpec(memory_space=pltpu.VMEM)
     hbm = pl.BlockSpec(memory_space=pl.ANY)
@@ -639,26 +671,31 @@
         main_kernel,
         out_shape=[
             jax.ShapeDtypeStruct(block, jnp.float32),
-            jax.ShapeDtypeStruct((8, LANES), jnp.int32),
+            jax.ShapeDtypeStruct((1,), jnp.int32),
         ],
-        in_specs=[smem, smem, smem, vmem, hbm, hbm, hbm, hbm, hbm],
-        out_specs=[vmem, vmem],
+        in_specs=[smem, vmem, vmem] + [hbm] * 7,
+        out_specs=[vmem, smem],
         scratch_shapes=[
+            pltpu.SMEM((8, TERMS), jnp.int32),
+            pltpu.SMEM((8, TERMS), jnp.int32),
+            pltpu.VMEM((8, LANES), jnp.int32),
             pltpu.VMEM(block, jnp.bfloat16),
             pltpu.VMEM(block, jnp.bfloat16),
             pltpu.VMEM((16, TW, TW), jnp.bfloat16),
             pltpu.VMEM((16, TW, TW), jnp.bfloat16),
             pltpu.VMEM((2, 2 * TW, 8 * TW), jnp.bfloat16),
             pltpu.VMEM((16, TW, TW), jnp.bfloat16),
-            pltpu.VMEM((TERMS, J, TW, TW), jnp.bfloat16),
-            pltpu.VMEM((CHUNKS, NX, CAP, ROWS, TW), jnp.bfloat16),
-            pltpu.VMEM((CHUNKS, NX * NC, CAP, ROWS, TW), jnp.bfloat16),
-            pltpu.VMEM((entries, ROWS, TW), jnp.bfloat16),
-            pltpu.VMEM((RING, LANES, ROWS, TW), jnp.float32),
-            pltpu.VMEM((CHUNKS, 2, 4, SLOTS, ROWS, TW), jnp.bfloat16),
-            pltpu.VMEM((CHUNKS, 2, 4, SLOTS, ROWS, TW), jnp.bfloat16),
+            pltpu.VMEM((J, TERMS, TW, TW), jnp.bfloat16),
+            pltpu.VMEM((STEPS, NX, NC, CAP, HALF, TW), jnp.bfloat16),
+            pltpu.VMEM((STEPS, NX * NC, CAP, HALF, TW), jnp.bfloat16),
+            pltpu.VMEM((entries, HALF, TW), jnp.bfloat16),
+            pltpu.VMEM((STEPS, entries, HALF, TW), jnp.float32),
+            pltpu.VMEM((STEPS, 2, 4, GOALS, HALF, TW), jnp.bfloat16),
+            pltpu.VMEM((STEPS, 2, 4, GOALS, HALF, TW), jnp.bfloat16),
             pltpu.VMEM((8, SLOTS, TW, TW), jnp.bfloat16),
             pltpu.VMEM((4,) + block, jnp.bfloat16),
+            pltpu.VMEM((STEPS, SLOTS, HALF, TW), jnp.float32),
+            pltpu.VMEM((STEPS, SLOTS, HALF, TW), jnp.float32),
             pltpu.VMEM((NX + 1, 8, LANES), jnp.int32),
             pltpu.VMEM((2, NX * NC, 8, LANES), jnp.int32),
             pltpu.VMEM((8, LANES), jnp.int32),
@@ -667,20 +704,22 @@
             pltpu.VMEM((8, LANES), jnp.int32),
             pltpu.SMEM((8, LANES), jnp.int32),
             pltpu.SMEM((8, LANES), jnp.int32),
-            dma((5,)),
-            dma((CHUNKS, NX)),
-            dma((CHUNKS, NX)),
-            dma((CHUNKS,)),
-            dma((CHUNKS, NX * NC)),
-            dma((CHUNKS, 2, 4)),
-            dma((CHUNKS, 2, 4)),
+            pltpu.SMEM((8, LANES), jnp.int32),
+            dma((7,)),
+            dma((STEPS, NX, NC)),
+            dma((STEPS,)),
+            dma((STEPS, NX * NC)),
+            dma((STEPS, 2, 4)),
+            dma((STEPS, 2, 4)),
             dma((4,)),
             dma((4,)),
             dma((2, NX * NC)),
             dma((2, NX * NC)),
             dma((NZ,)),
             dma((NZ,)),
-            dma((2,)),
+            dma((3,)),
+            dma((STEPS,)),
+            dma((STEPS,)),
         ],
         compiler_params=pltpu.CompilerParams(
             collective_id=0, has_side_effects=True, vmem_limit_bytes=58 * 2**20
@@ -688,7 +727,7 @@
         cost_estimate=pl.CostEstimate(
             flops=2 * 1024 * TW**3, bytes_accessed=8 * 2**20, transcendentals=0
         ),
-    )(sources, factors, blocks, keys, amplitudes, exchange, left, right, ints)
+    )(blocks, owners, slots, sources, factors, amplitudes, exchange, left, right, ints)
 
 
 def spilled(
@@ -729,10 +768,9 @@
     amplitudes, exchange_ints, left_factors, right_factors, ladder_sources, ladder_factors,
     dest_owners, dest_slots, cycle_blocks, cycle_ints,
 ):
-    keys = dest_owners[:, 0] * SLOTS + dest_slots
-    row = jnp.pad(keys, (0, LANES - TERMS))[None, :]
     total, flags = main_call(
-        ladder_sources, ladder_factors, cycle_blocks, row, amplitudes, exchange_ints,
+        ladder_sources.T, ladder_factors.T, cycle_blocks, dest_owners.reshape(1, TERMS),
+        dest_slots[None, :], amplitudes, exchange_ints,
         left_factors, right_factors, cycle_ints,
     )
 
@@ -740,12 +778,13 @@
         return total.astype(jnp.bfloat16)
 
     def more():
+        keys = dest_owners[:, 0] * SLOTS + dest_slots
         rest = spilled(
             amplitudes, left_factors, right_factors, ladder_sources, ladder_factors, keys
         )
         return (total + rest).astype(jnp.bfloat16)
 
-    return lax.cond(jnp.max(flags) > 0, more, whole)
+    return lax.cond(flags[0] > 0, more, whole)
 
 
 def solution(mesh):

time: 95.1 us -> 89.1 us (0.937)
  local copies, waits for them, and re-layouts: 3.28 us -> 0.03 us
  other arithmetic: 2.99 us -> 0.89 us
    unnamed x12 -> x14, local copies, waits for them, and re-layouts: 2.74 us -> 0.03 us
    reduce_max x1 -> x0, other arithmetic: 1.31 us -> none  [local(): return lax.cond(jnp.max(flags) > 0, more, whole)]
where the time goes in v3:
time: 89.1 us; the launch traced here: 89 us
  Pallas kernels  87.3 us (98%)
    pallas_call x1, Pallas kernels, main_call(): pl.pallas_call(main_kernel, out_shape=[jax.ShapeDtypeStruct(block, jnp.fl...  87.3 us

profile of v3, /device:TPU:1, one launch (start us, length us, event | category | flops | bytes accessed | tf_op | source)
XLA Modules:
  0.0 89.0 jit_solution(14230514259565731174)
XLA Ops:
  0.0 0.0 copy-start.4
  0.0 0.0 copy-start.3
  0.0 0.0 copy-start.2
  0.0 0.0 copy-start.1
  0.0 0.0 copy-start.7
  0.0 0.0 copy-start.6
  0.0 0.0 copy-start.5
  0.0 87.3 %shard_map.102 = (f32[2,8,128,128]{3,2,1,0:T(8,128)S(1)}, s32[1]{0:T(128)}) custom-call(s32[8]{0:T(128)} %blocks_ref.1, s32[1,32]{1,0:T(1,128)} %bitcast.18, s32[1,32]{1,0:T(1,128)} %bitcast.19, s32[8,32]{1,0:T(8,128)} %bitcast.15, s32[8,32]{1,0:T(8,128)} %bitcast.16, bf16[2,8,128,128]{3,2,1,0:T(8,128)(2,1)} %amp_hbm.1, bf16[2,8,128,128]{3,2,1,0:T(8,128)(2,1)} %exch_hbm.1, ...), custom_call_target="tpu_custom_call" | custom-call | flops 4294967296 | bytes 8388608 | tf_op jit(solution)/shard_map/pallas_call | solution.py:670
  88.0 0.0 copy-done.4
  88.1 0.0 copy-done.3
  88.1 0.0 copy-done.2
  88.1 0.0 copy-done.1
  88.1 0.0 copy-done.7
  88.1 0.0 copy-done.6
  88.1 0.0 copy-done.5
  88.1 0.9 convert_element_type.37
  (1 shorter events, 0.0 us)
Async XLA Ops:
  0.0 88.1 %copy-start.4 = (s32[32]{0:T(128)S(1)}, s32[32]{0:T(128)}, u32[]{:S(2)}) copy-start(s32[32]{0:T(128)} %param.19) | copy-start | bytes 388
  0.0 88.1 %copy-start.3 = (s32[32,1]{0,1:T(1,128)S(1)}, s32[32,1]{0,1:T(1,128)}, u32[]{:S(2)}) copy-start(s32[32,1]{0,1:T(1,128)} %param.18) | copy-start | bytes 388
  0.0 88.1 %copy-start.2 = (s32[32,8]{0,1:T(8,128)S(1)}, s32[32,8]{0,1:T(8,128)}, u32[]{:S(2)}) copy-start(s32[32,8]{0,1:T(8,128)} %param.17) | copy-start | bytes 3076
  0.0 88.1 %copy-start.1 = (s32[32,8]{0,1:T(8,128)S(1)}, s32[32,8]{0,1:T(8,128)}, u32[]{:S(2)}) copy-start(s32[32,8]{0,1:T(8,128)} %param.16) | copy-start | bytes 3076
  0.0 88.1 %copy-start.7 = (bf16[16,128,128]{2,1,0:T(8,128)(2,1)S(1)}, bf16[16,128,128]{2,1,0:T(8,128)(2,1)}, u32[]{:S(2)}) copy-start(bf16[16,128,128]{2,1,0:T(8,128)(2,1)} %right_hbm.1) | copy-start | bytes 1572868
  0.0 88.1 %copy-start.6 = (bf16[16,128,128]{2,1,0:T(8,128)(2,1)S(1)}, bf16[16,128,128]{2,1,0:T(8,128)(2,1)}, u32[]{:S(2)}) copy-start(bf16[16,128,128]{2,1,0:T(8,128)(2,1)} %left_hbm.1) | copy-start | bytes 1572868
  0.0 88.1 %copy-start.5 = (bf16[2,8,128,128]{3,2,1,0:T(8,128)(2,1)S(1)}, bf16[2,8,128,128]{3,2,1,0:T(8,128)(2,1)}, u32[]{:S(2)}) copy-start(bf16[2,8,128,128]{3,2,1,0:T(8,128)(2,1)} %amp_hbm.1) | copy-start | bytes 1572868
